TPU v7x, 256 devices: a whole 4x4x8 slice. The times are simulated.
256 devices in a mesh: dp: 2 (over core), seq: 128 (over z, x, y).
Axes of the slice: x: 4, y: 4, z: 8, core: 2. Of those that a mesh axis runs over, the one named last changes fastest.
Arguments:
- signal: bfloat16 [2, 16384, 512], P('dp', 'seq'), may hold values from -6 to 6
- grad_out: bfloat16 [2, 16384, 512], P('dp', 'seq'), may hold values from -6 to 6
- mode_coef: float32 [2, 2, 64, 512], replicated, may hold values from -6 to 6
- decay_param: float32 [2, 64, 512], replicated, may hold values from 0.1 to 370
- freq_index: int32 [2, 64, 512], replicated, may hold values from 0 to 4095
- skip_gain: float32 [512], replicated, may hold values from -4 to 4
Outputs:
- grad_signal: bfloat16 [2, 16384, 512], P('dp', 'seq')
- grad_coef: float32 [2, 2, 64, 512], replicated
- grad_skip: float32 [512], replicated
All inputs are finite; a program needn't handle non-finite values.
Results may differ from a plain program's by a relative error of at most 0.011.
Values may be sent and summed in bfloat16 or wider, within the bound.
A program may use at most 64 MiB of HBM per device.

v0:
```python
import math

import jax
import jax.numpy as jnp
from jax import lax
from jax.sharding import PartitionSpec as P

highest = lax.Precision.HIGHEST


def shortened(value):

    def short(part):
        return part.astype(jnp.bfloat16) if part.dtype == jnp.float32 else part

    return jax.tree.map(short, value)


def angle_pair(turns, period):
    angle = turns.astype(jnp.float32) * (2.0 * math.pi / period)
    return (jnp.cos(angle), jnp.sin(angle))


def exact_turns(freq_index, lag_list, period):
    lag_high = lag_list // 1024
    lag_low = lag_list % 1024
    return (freq_index * lag_high % period * 1024 + freq_index * lag_low) % period


def dft_table(row_count, col_count, period):
    row_idx = lax.broadcasted_iota(jnp.int32, (row_count, col_count), 0)
    col_idx = lax.broadcasted_iota(jnp.int32, (row_count, col_count), 1)
    return angle_pair(row_idx * col_idx % period, period)


def wide_groups(values):
    group_size = math.gcd(16, values.shape[0])
    return values.reshape(values.shape[0] // group_size, group_size, values.shape[1])


def fade_wave(decay_rate, freq_index, lag_list, period):
    turns = exact_turns(freq_index[:, None, :], lag_list[None, :, None], period)
    wave_cos, wave_sin = angle_pair(turns, period)
    fade_out = jnp.exp(-decay_rate[:, None, :] * lag_list[None, :, None].astype(jnp.float32))
    return (fade_out * wave_cos, fade_out * wave_sin)


def kernel_values(coef_dir, rate_dir, freq_dir, lag_list, period, kernel_scale):

    def kernel_mode_step(running, mode_slice):
        coef_re, coef_im, decay_rate, freq_group = mode_slice
        wave_cos, wave_sin = fade_wave(decay_rate, freq_group, lag_list, period)
        summed = jnp.sum(coef_re[:, None, :] * wave_cos - coef_im[:, None, :] * wave_sin, axis=0)
        return (running + summed, None)

    start_zero = jnp.zeros((lag_list.shape[0], coef_dir.shape[2]), jnp.float32)
    running, _ = lax.scan(
        kernel_mode_step,
        start_zero,
        (
            wide_groups(coef_dir[0]),
            wide_groups(coef_dir[1]),
            wide_groups(rate_dir),
            wide_groups(freq_dir),
        ),
    )
    return 2.0 * kernel_scale * running


def coef_gradient(weights, rate_dir, freq_dir, lag_list, period, kernel_scale):

    def coef_mode_step(carry, mode_slice):
        decay_rate, freq_group = mode_slice
        wave_cos, wave_sin = fade_wave(decay_rate, freq_group, lag_list, period)
        return (
            carry,
            jnp.stack(
                [
                    jnp.sum(weights[None] * wave_cos, axis=1),
                    -jnp.sum(weights[None] * wave_sin, axis=1),
                ]
            ),
        )

    _, rows_out = lax.scan(
        coef_mode_step, jnp.zeros((), jnp.float32), (wide_groups(rate_dir), wide_groups(freq_dir))
    )
    channels = weights.shape[1]
    return 2.0 * kernel_scale * jnp.swapaxes(rows_out, 0, 1).reshape(2, rate_dir.shape[0], channels)


def first_section(received, position, seq_count, width):
    sources = received.shape[1]
    rows_per = received.shape[2]
    period = 2 * seq_count * width
    cos_table, sin_table = dft_table(2 * seq_count, sources, 2 * seq_count)
    real_part = jnp.einsum("ks,gsrh->gkrh", cos_table, received, precision=highest)
    imag_part = -jnp.einsum("ks,gsrh->gkrh", sin_table, received, precision=highest)
    freq_idx = lax.broadcasted_iota(jnp.int32, (2 * seq_count, rows_per), 0)
    local_idx = position * rows_per + lax.broadcasted_iota(jnp.int32, (2 * seq_count, rows_per), 1)
    twist_cos, twist_sin = angle_pair(freq_idx * local_idx % period, period)
    twist_cos = twist_cos[None, :, :, None]
    twist_sin = twist_sin[None, :, :, None]
    return (
        real_part * twist_cos + imag_part * twist_sin,
        imag_part * twist_cos - real_part * twist_sin,
    )


def signal_first(stacked, position, seq_count, width):
    return first_section(
        lax.all_to_all(stacked[:, None], "seq", split_axis=2, concat_axis=1, tiled=True).astype(
            jnp.float32
        ),
        position,
        seq_count,
        width,
    )


def spectrum_turn(first_re, first_im, width):
    cos_table, sin_table = dft_table(width, width, width)
    part_re = lax.all_to_all(
        first_re.astype(jnp.bfloat16), "seq", split_axis=1, concat_axis=2, tiled=True
    ).astype(first_re.dtype)
    part_im = lax.all_to_all(
        first_im.astype(jnp.bfloat16), "seq", split_axis=1, concat_axis=2, tiled=True
    ).astype(first_im.dtype)
    out_re = jnp.einsum("kt,gqth->gqkh", cos_table, part_re, precision=highest) + jnp.einsum(
        "kt,gqth->gqkh", sin_table, part_im, precision=highest
    )
    out_im = jnp.einsum("kt,gqth->gqkh", cos_table, part_im, precision=highest) - jnp.einsum(
        "kt,gqth->gqkh", sin_table, part_re, precision=highest
    )
    return (out_re, out_im)


def kernel_first(mode_coef, decay_rate, freq_index, position, seq_count, width, kernel_scale):
    length = width * seq_count
    rows_per = width // seq_count
    channels = mode_coef.shape[3]
    block_idx = lax.broadcasted_iota(jnp.int32, (seq_count, rows_per), 0)
    inner_idx = lax.broadcasted_iota(jnp.int32, (seq_count, rows_per), 1)
    lag_list = (block_idx * width + position * rows_per + inner_idx).reshape(-1)
    lower_half = kernel_values(
        mode_coef[0], decay_rate[0], freq_index[0], lag_list, length, kernel_scale
    )
    upper_lags = length - lag_list
    live_mask = (upper_lags < length).astype(jnp.float32)[:, None]
    upper_half = (
        kernel_values(mode_coef[1], decay_rate[1], freq_index[1], upper_lags, length, kernel_scale)
        * live_mask
    )
    stacked = jnp.concatenate([lower_half, upper_half], axis=0).reshape(
        1, 2 * seq_count, rows_per, channels
    )
    return first_section(stacked, position, seq_count, width)


def inverse_path(spec_re, spec_im, row_count, position, seq_count, width):
    rows_per = width // seq_count
    period = 2 * seq_count * width
    cos_table, sin_table = dft_table(width, width, width)
    head_re = jnp.einsum("tk,gqkh->gqth", cos_table, spec_re, precision=highest) - jnp.einsum(
        "tk,gqkh->gqth", sin_table, spec_im, precision=highest
    )
    head_im = jnp.einsum("tk,gqkh->gqth", cos_table, spec_im, precision=highest) + jnp.einsum(
        "tk,gqkh->gqth", sin_table, spec_re, precision=highest
    )
    back_cos, back_sin = dft_table(row_count, 2 * seq_count, 2 * seq_count)
    part_re = lax.all_to_all(
        shortened(head_re), "seq", split_axis=2, concat_axis=1, tiled=True
    ).astype(head_re.dtype)
    part_im = lax.all_to_all(
        shortened(head_im), "seq", split_axis=2, concat_axis=1, tiled=True
    ).astype(head_im.dtype)
    freq_idx = lax.broadcasted_iota(jnp.int32, (2 * seq_count, rows_per), 0)
    local_idx = position * rows_per + lax.broadcasted_iota(jnp.int32, (2 * seq_count, rows_per), 1)
    twist_cos, twist_sin = angle_pair(freq_idx * local_idx % period, period)
    twist_cos = twist_cos[None, :, :, None]
    twist_sin = twist_sin[None, :, :, None]
    turned_re = part_re * twist_cos - part_im * twist_sin
    turned_im = part_im * twist_cos + part_re * twist_sin
    values = jnp.einsum("sk,gkrh->gsrh", back_cos, turned_re, precision=highest) - jnp.einsum(
        "sk,gkrh->gsrh", back_sin, turned_im, precision=highest
    )
    moved = values * (1.0 / period)
    group_count = moved.shape[0]
    channels = moved.shape[3]
    shaped = moved.reshape(group_count, row_count // seq_count, seq_count, rows_per, channels)
    placed = lax.all_to_all(
        shortened(shaped), "seq", split_axis=2, concat_axis=3, tiled=True
    ).astype(shaped.dtype)
    return placed.reshape(group_count, row_count // seq_count, width, channels)


def on_device(signal, grad_out, mode_coef, decay_param, freq_index, skip_gain):
    seq_count = lax.axis_size("seq")
    position = lax.axis_index("seq")
    width = signal.shape[1]
    mode_count = decay_param.shape[1]
    length = width * seq_count
    kernel_scale = (mode_count * length) ** (-0.5)
    decay_rate = decay_param / float(length)
    kernel_parts = kernel_first(
        mode_coef, decay_rate, freq_index, position, seq_count, width, kernel_scale
    )
    first_re, first_im = signal_first(signal, position, seq_count, width)
    spec_re, spec_im = spectrum_turn(first_re, first_im, width)
    signal_re, signal_im = (spec_re[0], spec_im[0])
    first_re, first_im = signal_first(grad_out, position, seq_count, width)
    spec_re, spec_im = spectrum_turn(first_re, first_im, width)
    cotan_re, cotan_im = (spec_re[0], spec_im[0])
    spec_re, spec_im = spectrum_turn(kernel_parts[0], kernel_parts[1], width)
    kernel_found = (spec_re[0], spec_im[0])
    kernel_re, kernel_im = kernel_found
    through_re = cotan_re * kernel_re + cotan_im * kernel_im
    through_im = cotan_im * kernel_re - cotan_re * kernel_im
    corr_re = cotan_re * signal_re + cotan_im * signal_im
    corr_im = cotan_im * signal_re - cotan_re * signal_im
    through_pos = inverse_path(
        through_re[None], through_im[None], seq_count, position, seq_count, width
    )[0, 0]
    kernel_grad = inverse_path(
        corr_re[None], corr_im[None], 2 * seq_count, position, seq_count, width
    )[0]
    lag_low = position * width + lax.iota(jnp.int32, width)
    lag_high = length - lag_low
    live_mask = (lag_high < length).astype(jnp.float32)[:, None]
    grad_local = jnp.stack(
        [
            coef_gradient(
                kernel_grad[0], decay_rate[0], freq_index[0], lag_low, length, kernel_scale
            ),
            coef_gradient(
                kernel_grad[1] * live_mask,
                decay_rate[1],
                freq_index[1],
                lag_high,
                length,
                kernel_scale,
            ),
        ]
    )
    cotangent = grad_out[0].astype(jnp.float32)
    signal_value = signal[0].astype(jnp.float32)
    grad_signal = (through_pos + skip_gain[None, :] * cotangent).astype(jnp.bfloat16)[None]
    skip_local = jnp.sum(cotangent * signal_value, axis=0)
    grad_coef, grad_skip = lax.psum((grad_local, skip_local), ("dp", "seq"))
    return (grad_signal, grad_coef, grad_skip)


def solution(mesh):
    return jax.shard_map(
        on_device,
        mesh=mesh,
        in_specs=(P("dp", "seq", None), P("dp", "seq", None), P(), P(), P(), P()),
        out_specs=(P("dp", "seq", None), P(), P()),
        check_vma=False,
    )
```

profile of v0, /device:TPU:1, one launch (start us, length us, event | category | flops | bytes accessed | tf_op | source)
XLA Modules:
  0.0 908.4 jit_solution(1236299130199292765)
XLA Ops:
  10.9 16.5 %all-to-all-start.8 = ((bf16[128,2,256]{2,1,0:T(2,128)(2,1)}), bf16[128,2,256]{2,1,0:T(2,128)(2,1)S(1)}, u32[]{:S(2)}, u32[]{:S(2)}) async-start(bf16[128,2,256]{2,1,0:T(2,128)(2,1)} %reshape.971), calls=%async_computation.8 | async-start | bytes 262144 | tf_op jit(solution)/shard_map/all_to_all | solution.py:112
  29.4 80.0 %while.68 = (s32[]{:T(128)}, f32[128,512]{1,0:T(8,128)S(1)}, f32[4,16,512]{2,1,0:T(8,128)S(1)}, f32[4,16,512]{2,1,0:T(8,128)S(1)}, s32[4,16,512]{2,1,0:T(8,128)S...) while((s32[]{:T(128)}, f32[128,512]{1,0:T(8,128)S(1)}, ...), condition=%wide.region_2.3_spmd.clone.clone.clone, body=%wide.region_0.2_spmd.clone.clone.clone.sunk | while | flops 36778240 | bytes 1444987 | solution.py:57
  29.5 19.8 %subtract_reduce_fusion.4 = f32[128,512]{1,0:T(8,128)S(1)} fusion(f32[16,512]{1,0:T(8,128)S(1)} %get-tuple-element.1321, s32[128]{0:T(128)S(1)} %get-tuple-element.1322, s32[128]{0:T(128)S(1)} %get-tuple-element.1323, s32[16,512]{1,0:T(8,128)S(1)} %dynamic-slice_bitcast_fusion.19, f32[128]{0:T(128)S(1)} %convert_bitcast_fusion.14, ...), kind=kLoop, calls=%fused_computation.102.clone.1 | loop fusion | flops 36634624 | bytes 394752 | tf_op jit(solution)/shard_map/while/body/eval_jaxpr/reduce_sum | solution.py:53
  49.5 19.8 %subtract_reduce_fusion.4 = f32[128,512]{1,0:T(8,128)S(1)} fusion(f32[16,512]{1,0:T(8,128)S(1)} %get-tuple-element.1321, s32[128]{0:T(128)S(1)} %get-tuple-element.1322, s32[128]{0:T(128)S(1)} %get-tuple-element.1323, s32[16,512]{1,0:T(8,128)S(1)} %dynamic-slice_bitcast_fusion.19, f32[128]{0:T(128)S(1)} %convert_bitcast_fusion.14, ...), kind=kLoop, calls=%fused_computation.102.clone.1 | loop fusion | flops 36634624 | bytes 394752 | tf_op jit(solution)/shard_map/while/body/eval_jaxpr/reduce_sum | solution.py:53
  69.5 19.8 %subtract_reduce_fusion.4 = f32[128,512]{1,0:T(8,128)S(1)} fusion(f32[16,512]{1,0:T(8,128)S(1)} %get-tuple-element.1321, s32[128]{0:T(128)S(1)} %get-tuple-element.1322, s32[128]{0:T(128)S(1)} %get-tuple-element.1323, s32[16,512]{1,0:T(8,128)S(1)} %dynamic-slice_bitcast_fusion.19, f32[128]{0:T(128)S(1)} %convert_bitcast_fusion.14, ...), kind=kLoop, calls=%fused_computation.102.clone.1 | loop fusion | flops 36634624 | bytes 394752 | tf_op jit(solution)/shard_map/while/body/eval_jaxpr/reduce_sum | solution.py:53
  89.5 19.8 %subtract_reduce_fusion.4 = f32[128,512]{1,0:T(8,128)S(1)} fusion(f32[16,512]{1,0:T(8,128)S(1)} %get-tuple-element.1321, s32[128]{0:T(128)S(1)} %get-tuple-element.1322, s32[128]{0:T(128)S(1)} %get-tuple-element.1323, s32[16,512]{1,0:T(8,128)S(1)} %dynamic-slice_bitcast_fusion.19, f32[128]{0:T(128)S(1)} %convert_bitcast_fusion.14, ...), kind=kLoop, calls=%fused_computation.102.clone.1 | loop fusion | flops 36634624 | bytes 394752 | tf_op jit(solution)/shard_map/while/body/eval_jaxpr/reduce_sum | solution.py:53
  110.1 80.4 %while.69 = (s32[]{:T(128)}, f32[128,512]{1,0:T(8,128)S(1)}, f32[4,16,512]{2,1,0:T(8,128)S(1)}, f32[4,16,512]{2,1,0:T(8,128)S(1)}, s32[4,16,512]{2,1,0:T(8,128)S...) while((s32[]{:T(128)}, f32[128,512]{1,0:T(8,128)S(1)}, ...), condition=%wide.region_5.6_spmd.clone.clone.clone, body=%wide.region_3.5_spmd.clone.clone.clone.sunk | while | flops 36778368 | bytes 1444987 | solution.py:57
  110.6 19.8 %subtract_reduce_fusion.5 = f32[128,512]{1,0:T(8,128)S(1)} fusion(f32[16,512]{1,0:T(8,128)S(1)} %get-tuple-element.1332, s32[128]{0:T(128)S(1)} %get-tuple-element.1333, s32[128]{0:T(128)S(1)} %get-tuple-element.1334, s32[16,512]{1,0:T(8,128)S(1)} %dynamic-slice_bitcast_fusion.22, f32[128]{0:T(128)S(1)} %convert_bitcast_fusion.15, ...), kind=kLoop, calls=%fused_computation.134.clone.1 | loop fusion | flops 36634624 | bytes 394752 | tf_op jit(solution)/shard_map/while/body/eval_jaxpr/reduce_sum | solution.py:53
  130.6 19.8 %subtract_reduce_fusion.5 = f32[128,512]{1,0:T(8,128)S(1)} fusion(f32[16,512]{1,0:T(8,128)S(1)} %get-tuple-element.1332, s32[128]{0:T(128)S(1)} %get-tuple-element.1333, s32[128]{0:T(128)S(1)} %get-tuple-element.1334, s32[16,512]{1,0:T(8,128)S(1)} %dynamic-slice_bitcast_fusion.22, f32[128]{0:T(128)S(1)} %convert_bitcast_fusion.15, ...), kind=kLoop, calls=%fused_computation.134.clone.1 | loop fusion | flops 36634624 | bytes 394752 | tf_op jit(solution)/shard_map/while/body/eval_jaxpr/reduce_sum | solution.py:53
  150.7 19.8 %subtract_reduce_fusion.5 = f32[128,512]{1,0:T(8,128)S(1)} fusion(f32[16,512]{1,0:T(8,128)S(1)} %get-tuple-element.1332, s32[128]{0:T(128)S(1)} %get-tuple-element.1333, s32[128]{0:T(128)S(1)} %get-tuple-element.1334, s32[16,512]{1,0:T(8,128)S(1)} %dynamic-slice_bitcast_fusion.22, f32[128]{0:T(128)S(1)} %convert_bitcast_fusion.15, ...), kind=kLoop, calls=%fused_computation.134.clone.1 | loop fusion | flops 36634624 | bytes 394752 | tf_op jit(solution)/shard_map/while/body/eval_jaxpr/reduce_sum | solution.py:53
  170.7 19.8 %subtract_reduce_fusion.5 = f32[128,512]{1,0:T(8,128)S(1)} fusion(f32[16,512]{1,0:T(8,128)S(1)} %get-tuple-element.1332, s32[128]{0:T(128)S(1)} %get-tuple-element.1333, s32[128]{0:T(128)S(1)} %get-tuple-element.1334, s32[16,512]{1,0:T(8,128)S(1)} %dynamic-slice_bitcast_fusion.22, f32[128]{0:T(128)S(1)} %convert_bitcast_fusion.15, ...), kind=kLoop, calls=%fused_computation.134.clone.1 | loop fusion | flops 36634624 | bytes 394752 | tf_op jit(solution)/shard_map/while/body/eval_jaxpr/reduce_sum | solution.py:53
  193.8 1.6 convolution_bitcast_fusion.1
  195.4 1.6 fusion.75
  197.1 13.5 %all-to-all-start = ((bf16[128,2,256]{2,1,0:T(2,128)(2,1)}), bf16[128,2,256]{2,1,0:T(2,128)(2,1)S(1)}, u32[]{:S(2)}, u32[]{:S(2)}) async-start(bf16[128,2,256]{2,1,0:T(2,128)(2,1)} %reshape.959), calls=%async_computation | async-start | bytes 262144 | tf_op jit(solution)/shard_map/all_to_all | solution.py:112
  211.5 1.6 fusion.74
  213.1 8.7 all-to-all-done
  224.6 2.2 reduce.20
  227.6 6.2 all-to-all-start.3
  234.2 2.2 reduce.19
  237.2 9.2 %all-to-all-done.3 = bf16[128,2,512]{2,1,0:T(2,128)(2,1)S(1)} async-done(((bf16[128,2,512]{2,1,0:T(2,128)(2,1)}), bf16[128,2,512]{2,1,0:T(2,128)(2,1)S(1)}, u32[]{:S(2)}, u32[]{:S(2)}) %all-to-all-start.3) | async-done | bytes 262176 | tf_op jit(solution)/shard_map/all_to_all | solution.py:123
  246.4 6.2 all-to-all-start.4
  253.0 2.2 reduce.16
  256.0 9.2 %all-to-all-done.4 = bf16[128,2,512]{2,1,0:T(2,128)(2,1)S(1)} async-done(((bf16[128,2,512]{2,1,0:T(2,128)(2,1)}), bf16[128,2,512]{2,1,0:T(2,128)(2,1)S(1)}, u32[]{:S(2)}, u32[]{:S(2)}) %all-to-all-start.4) | async-done | bytes 262176 | tf_op jit(solution)/shard_map/all_to_all | solution.py:126
  265.2 6.6 all-to-all-start.9
  272.2 2.2 reduce.15
  275.6 2.2 reduce.17
  279.0 2.2 reduce.18
  282.5 1.5 bitcast_reduce_fusion.2
  284.0 1.5 bitcast_reduce_fusion.3
  285.5 13.5 %all-to-all-start.10 = ((bf16[128,2,512]{2,1,0:T(2,128)(2,1)}), bf16[128,2,512]{2,1,0:T(2,128)(2,1)S(1)}, u32[]{:S(2)}, u32[]{:S(2)}) async-start(bf16[128,2,512]{2,1,0:T(2,128)(2,1)} %reshape.973), calls=%async_computation.10 | async-start | bytes 524288 | tf_op jit(solution)/shard_map/all_to_all | solution.py:126
  299.3 1.5 bitcast_reduce_fusion
  302.7 8.9 all-to-all-done.10
  311.6 6.2 all-to-all-start.1
  318.1 1.5 bitcast_reduce_fusion.1
  322.3 8.1 all-to-all-done.1
  330.4 6.4 all-to-all-start.2
  337.0 1.5 bitcast_reduce_fusion.5
  343.8 5.6 all-to-all-done.2
  357.7 7.7 all-to-all-start.11
  368.0 10.1 %all-to-all-done.11 = bf16[1,2,128,512]{3,1,0,2:T(2,128)(2,1)S(1)} async-done(((bf16[1,2,128,512]{3,1,0,2:T(2,128)(2,1)}), bf16[1,2,128,512]{3,1,0,2:T(2,128)(2,1)S(1)}, u32[]{:S(2)}, u32[]{:S(2)}) %all-to-all-start.11) | async-done | bytes 262176 | tf_op jit(solution)/shard_map/all_to_all | solution.py:171
  378.1 6.2 all-to-all-start.12
  387.6 9.3 %all-to-all-done.12 = bf16[1,2,128,512]{3,1,0,2:T(2,128)(2,1)S(1)} async-done(((bf16[1,2,128,512]{3,1,0,2:T(2,128)(2,1)}), bf16[1,2,128,512]{3,1,0,2:T(2,128)(2,1)S(1)}, u32[]{:S(2)}, u32[]{:S(2)}) %all-to-all-start.12) | async-done | bytes 262176 | tf_op jit(solution)/shard_map/all_to_all | solution.py:174
  396.9 6.2 all-to-all-start.5
  405.9 9.8 %all-to-all-done.5 = bf16[1,2,128,512]{3,1,0,2:T(2,128)(2,1)S(1)} async-done(((bf16[1,2,128,512]{3,1,0,2:T(2,128)(2,1)}), bf16[1,2,128,512]{3,1,0,2:T(2,128)(2,1)S(1)}, u32[]{:S(2)}, u32[]{:S(2)}) %all-to-all-start.5) | async-done | bytes 262176 | tf_op jit(solution)/shard_map/all_to_all | solution.py:171
  415.7 6.3 all-to-all-start.6
  422.0 1.7 fusion.105
  423.7 1.7 fusion.78
  426.6 8.0 all-to-all-done.6
  434.6 6.2 all-to-all-start.13
  446.9 6.5 all-to-all-done.13
  453.4 6.7 all-to-all-start.7
  460.8 88.0 %while.66 = (s32[]{:T(128)}, f32[4,2,16,512]{3,2,1,0:T(8,128)S(1)}, f32[1,128,512]{2,1,0:T(8,128)S(1)}, f32[4,16,512]{2,1,0:T(8,128)}, s32[4,16,512]{2,1,0:T(8,128)}, /*index=5*/s32[]{:T(128)}, s32[]{:T(128)}) while((s32[]{:T(128)}, f32[4,2,16,512]{3,2,1,0:T(8,128)S(1)}, f32[1,128,512]{2,1,0:T(8,128)S(1)}, ...), condition=%wide.region_9.10_spmd.clone.clone, body=%wide.region_6.9_spmd.clone.clone.sunk | while | flops 36720256 | bytes 724065 | solution.py:85
  462.6 20.3 %multiply_reduce_fusion.6 = (f32[16,512]{1,0:T(8,128)S(1)}, f32[16,512]{1,0:T(8,128)S(1)}) fusion(s32[128]{0:T(128)S(1)} %get-tuple-element.1300, s32[128]{0:T(128)S(1)} %get-tuple-element.1301, s32[16,512]{1,0:T(8,128)S(1)} %dynamic-slice_bitcast_fusion.16, f32[128]{0:T(128)S(1)} %convert_bitcast_fusion.12, f32[16,512]{1,0:T(8,128)S(1)} %negate_bitcast_fusion.10, ...), kind=kLoop, calls=%fused_computation.35.clone.1 | loop fusion | flops 36683776 | bytes 394752 | tf_op jit(solution)/shard_map/while/body/eval_jaxpr/reduce_sum | solution.py:79
  484.6 20.3 %multiply_reduce_fusion.6 = (f32[16,512]{1,0:T(8,128)S(1)}, f32[16,512]{1,0:T(8,128)S(1)}) fusion(s32[128]{0:T(128)S(1)} %get-tuple-element.1300, s32[128]{0:T(128)S(1)} %get-tuple-element.1301, s32[16,512]{1,0:T(8,128)S(1)} %dynamic-slice_bitcast_fusion.16, f32[128]{0:T(128)S(1)} %convert_bitcast_fusion.12, f32[16,512]{1,0:T(8,128)S(1)} %negate_bitcast_fusion.10, ...), kind=kLoop, calls=%fused_computation.35.clone.1 | loop fusion | flops 36683776 | bytes 394752 | tf_op jit(solution)/shard_map/while/body/eval_jaxpr/reduce_sum | solution.py:79
  506.5 20.3 %multiply_reduce_fusion.6 = (f32[16,512]{1,0:T(8,128)S(1)}, f32[16,512]{1,0:T(8,128)S(1)}) fusion(s32[128]{0:T(128)S(1)} %get-tuple-element.1300, s32[128]{0:T(128)S(1)} %get-tuple-element.1301, s32[16,512]{1,0:T(8,128)S(1)} %dynamic-slice_bitcast_fusion.16, f32[128]{0:T(128)S(1)} %convert_bitcast_fusion.12, f32[16,512]{1,0:T(8,128)S(1)} %negate_bitcast_fusion.10, ...), kind=kLoop, calls=%fused_computation.35.clone.1 | loop fusion | flops 36683776 | bytes 394752 | tf_op jit(solution)/shard_map/while/body/eval_jaxpr/reduce_sum | solution.py:79
  528.4 20.3 %multiply_reduce_fusion.6 = (f32[16,512]{1,0:T(8,128)S(1)}, f32[16,512]{1,0:T(8,128)S(1)}) fusion(s32[128]{0:T(128)S(1)} %get-tuple-element.1300, s32[128]{0:T(128)S(1)} %get-tuple-element.1301, s32[16,512]{1,0:T(8,128)S(1)} %dynamic-slice_bitcast_fusion.16, f32[128]{0:T(128)S(1)} %convert_bitcast_fusion.12, f32[16,512]{1,0:T(8,128)S(1)} %negate_bitcast_fusion.10, ...), kind=kLoop, calls=%fused_computation.35.clone.1 | loop fusion | flops 36683776 | bytes 394752 | tf_op jit(solution)/shard_map/while/body/eval_jaxpr/reduce_sum | solution.py:79
  549.0 84.8 %while.67 = (s32[]{:T(128)}, f32[4,2,16,512]{3,2,1,0:T(8,128)S(1)}, f32[128,512]{1,0:T(8,128)S(1)}, f32[4,16,512]{2,1,0:T(8,128)}, s32[4,16,512]{2,1,0:T(8,128)S(1)}, /*index=5*/s32[]{:T(128)}, s32[]{:T(128)}) while((s32[]{:T(128)}, f32[4,2,16,512]{3,2,1,0:T(8,128)S(1)}, f32[128,512]{1,0:T(8,128)S(1)}, ...), condition=%wide.region_13.14_spmd.clone.clone, body=%wide.region_10.13_spmd.clone.clone.sunk | while | flops 36720640 | bytes 724065 | solution.py:85
  549.8 20.3 %multiply_reduce_fusion.7 = (f32[16,512]{1,0:T(8,128)S(1)}, f32[16,512]{1,0:T(8,128)S(1)}) fusion(s32[128]{0:T(128)S(1)} %get-tuple-element.1310, s32[128]{0:T(128)S(1)} %get-tuple-element.1311, s32[16,512]{1,0:T(8,128)S(1)} %dynamic-slice_bitcast_fusion.17, f32[128]{0:T(128)S(1)} %convert_bitcast_fusion.13, f32[16,512]{1,0:T(8,128)S(1)} %negate_bitcast_fusion.12, ...), kind=kLoop, calls=%fused_computation.69.clone.1 | loop fusion | flops 36683776 | bytes 394752 | tf_op jit(solution)/shard_map/while/body/eval_jaxpr/reduce_sum | solution.py:79
  571.0 20.3 %multiply_reduce_fusion.7 = (f32[16,512]{1,0:T(8,128)S(1)}, f32[16,512]{1,0:T(8,128)S(1)}) fusion(s32[128]{0:T(128)S(1)} %get-tuple-element.1310, s32[128]{0:T(128)S(1)} %get-tuple-element.1311, s32[16,512]{1,0:T(8,128)S(1)} %dynamic-slice_bitcast_fusion.17, f32[128]{0:T(128)S(1)} %convert_bitcast_fusion.13, f32[16,512]{1,0:T(8,128)S(1)} %negate_bitcast_fusion.12, ...), kind=kLoop, calls=%fused_computation.69.clone.1 | loop fusion | flops 36683776 | bytes 394752 | tf_op jit(solution)/shard_map/while/body/eval_jaxpr/reduce_sum | solution.py:79
  592.2 20.3 %multiply_reduce_fusion.7 = (f32[16,512]{1,0:T(8,128)S(1)}, f32[16,512]{1,0:T(8,128)S(1)}) fusion(s32[128]{0:T(128)S(1)} %get-tuple-element.1310, s32[128]{0:T(128)S(1)} %get-tuple-element.1311, s32[16,512]{1,0:T(8,128)S(1)} %dynamic-slice_bitcast_fusion.17, f32[128]{0:T(128)S(1)} %convert_bitcast_fusion.13, f32[16,512]{1,0:T(8,128)S(1)} %negate_bitcast_fusion.12, ...), kind=kLoop, calls=%fused_computation.69.clone.1 | loop fusion | flops 36683776 | bytes 394752 | tf_op jit(solution)/shard_map/while/body/eval_jaxpr/reduce_sum | solution.py:79
  613.4 20.3 %multiply_reduce_fusion.7 = (f32[16,512]{1,0:T(8,128)S(1)}, f32[16,512]{1,0:T(8,128)S(1)}) fusion(s32[128]{0:T(128)S(1)} %get-tuple-element.1310, s32[128]{0:T(128)S(1)} %get-tuple-element.1311, s32[16,512]{1,0:T(8,128)S(1)} %dynamic-slice_bitcast_fusion.17, f32[128]{0:T(128)S(1)} %convert_bitcast_fusion.13, f32[16,512]{1,0:T(8,128)S(1)} %negate_bitcast_fusion.12, ...), kind=kLoop, calls=%fused_computation.69.clone.1 | loop fusion | flops 36683776 | bytes 394752 | tf_op jit(solution)/shard_map/while/body/eval_jaxpr/reduce_sum | solution.py:79
  636.9 88.4 %psum.15 = f32[512]{0:T(512)} all-reduce(f32[512]{0:T(512)S(1)} %get-tuple-element.1134), channel_id=1, replica_groups=mesh['dp'=2,'seq'=128] {'dp','seq'}, use_global_device_ids=true, to_apply=%region_16.17 | all-reduce | flops 512 | bytes 4096 | tf_op jit(solution)/shard_map/psum | solution.py:249
  725.3 174.2 %all-reduce.2.cloned.1.call-done = f32[2,2,64,512]{3,2,1,0:T(8,128)} async-done(((f32[2,2,64,512]{3,2,1,0:T(8,128)}), f32[2,2,64,512]{3,2,1,0:T(8,128)}) %all-reduce.2.cloned.1.call-update) | async-done | bytes 524304 | tf_op jit(solution)/shard_map/psum | solution.py:249
  899.5 1.9 copy.205
  (236 shorter events, 69.7 us)
Async XLA Ops:
  8.3 19.2 %copy-start.7 = (f32[2,2,64,512]{3,2,1,0:T(8,128)S(1)}, f32[2,2,64,512]{3,2,1,0:T(8,128)}, u32[]{:S(2)}) copy-start(f32[2,2,64,512]{3,2,1,0:T(8,128)} %param.16) | copy-start | bytes 1572868
  10.9 186.2 %all-to-all-start.8 = ((bf16[128,2,256]{2,1,0:T(2,128)(2,1)}), bf16[128,2,256]{2,1,0:T(2,128)(2,1)S(1)}, u32[]{:S(2)}, u32[]{:S(2)}) async-start(bf16[128,2,256]{2,1,0:T(2,128)(2,1)} %reshape.971), calls=%async_computation.8 | async-start | bytes 262144 | tf_op jit(solution)/shard_map/all_to_all | solution.py:112
  27.5 1.0 copy-start.12
  28.4 0.9 copy-start.13
  109.4 0.7 copy-start.4
  109.5 0.7 copy-start.6
  190.6 0.6 copy-start.5
  190.6 1.0 copy-start.9
  197.1 24.7 %all-to-all-start = ((bf16[128,2,256]{2,1,0:T(2,128)(2,1)}), bf16[128,2,256]{2,1,0:T(2,128)(2,1)S(1)}, u32[]{:S(2)}, u32[]{:S(2)}) async-start(bf16[128,2,256]{2,1,0:T(2,128)(2,1)} %reshape.959), calls=%async_computation | async-start | bytes 262144 | tf_op jit(solution)/shard_map/all_to_all | solution.py:112
  221.9 1.0 copy-start.11
  227.6 18.8 %all-to-all-start.3 = ((bf16[128,2,512]{2,1,0:T(2,128)(2,1)}), bf16[128,2,512]{2,1,0:T(2,128)(2,1)S(1)}, u32[]{:S(2)}, u32[]{:S(2)}) async-start(bf16[128,2,512]{2,1,0:T(2,128)(2,1)} %reshape.967), calls=%async_computation.3 | async-start | bytes 524288 | tf_op jit(solution)/shard_map/all_to_all | solution.py:123
  246.4 18.8 %all-to-all-start.4 = ((bf16[128,2,512]{2,1,0:T(2,128)(2,1)}), bf16[128,2,512]{2,1,0:T(2,128)(2,1)S(1)}, u32[]{:S(2)}, u32[]{:S(2)}) async-start(bf16[128,2,512]{2,1,0:T(2,128)(2,1)} %reshape.965), calls=%async_computation.4 | async-start | bytes 524288 | tf_op jit(solution)/shard_map/all_to_all | solution.py:126
  265.2 20.4 %all-to-all-start.9 = ((bf16[128,2,512]{2,1,0:T(2,128)(2,1)}), bf16[128,2,512]{2,1,0:T(2,128)(2,1)S(1)}, u32[]{:S(2)}, u32[]{:S(2)}) async-start(bf16[128,2,512]{2,1,0:T(2,128)(2,1)} %reshape.975), calls=%async_computation.9 | async-start | bytes 524288 | tf_op jit(solution)/shard_map/all_to_all | solution.py:123
  285.5 26.1 %all-to-all-start.10 = ((bf16[128,2,512]{2,1,0:T(2,128)(2,1)}), bf16[128,2,512]{2,1,0:T(2,128)(2,1)S(1)}, u32[]{:S(2)}, u32[]{:S(2)}) async-start(bf16[128,2,512]{2,1,0:T(2,128)(2,1)} %reshape.973), calls=%async_computation.10 | async-start | bytes 524288 | tf_op jit(solution)/shard_map/all_to_all | solution.py:126
  311.6 18.8 %all-to-all-start.1 = ((bf16[128,2,512]{2,1,0:T(2,128)(2,1)}), bf16[128,2,512]{2,1,0:T(2,128)(2,1)S(1)}, u32[]{:S(2)}, u32[]{:S(2)}) async-start(bf16[128,2,512]{2,1,0:T(2,128)(2,1)} %reshape.961), calls=%async_computation.1 | async-start | bytes 524288 | tf_op jit(solution)/shard_map/all_to_all | solution.py:123
  330.4 19.0 %all-to-all-start.2 = ((bf16[128,2,512]{2,1,0:T(2,128)(2,1)}), bf16[128,2,512]{2,1,0:T(2,128)(2,1)S(1)}, u32[]{:S(2)}, u32[]{:S(2)}) async-start(bf16[128,2,512]{2,1,0:T(2,128)(2,1)} %reshape.963), calls=%async_computation.2 | async-start | bytes 524288 | tf_op jit(solution)/shard_map/all_to_all | solution.py:126
  351.5 1.0 copy-start
  352.5 1.3 copy-start.3
  353.1 1.1 copy-start.1
  353.2 1.2 copy-start.2
  357.7 20.4 %all-to-all-start.11 = ((bf16[1,2,128,512]{3,1,0,2:T(2,128)(2,1)}), bf16[1,2,128,512]{3,1,0,2:T(2,128)(2,1)S(1)}, u32[]{:S(2)}, u32[]{:S(2)}) async-start(bf16[1,2,128,512]{3,1,0,2:T(2,128)(2,1)} %copy.107), calls=%async_computation.11 | async-start | bytes 524288 | tf_op jit(solution)/shard_map/all_to_all | solution.py:171
  378.1 18.8 %all-to-all-start.12 = ((bf16[1,2,128,512]{3,1,0,2:T(2,128)(2,1)}), bf16[1,2,128,512]{3,1,0,2:T(2,128)(2,1)S(1)}, u32[]{:S(2)}, u32[]{:S(2)}) async-start(bf16[1,2,128,512]{3,1,0,2:T(2,128)(2,1)} %copy.108), calls=%async_computation.12 | async-start | bytes 524288 | tf_op jit(solution)/shard_map/all_to_all | solution.py:174
  396.9 18.8 %all-to-all-start.5 = ((bf16[1,2,128,512]{3,1,0,2:T(2,128)(2,1)}), bf16[1,2,128,512]{3,1,0,2:T(2,128)(2,1)S(1)}, u32[]{:S(2)}, u32[]{:S(2)}) async-start(bf16[1,2,128,512]{3,1,0,2:T(2,128)(2,1)} %copy.98), calls=%async_computation.5 | async-start | bytes 524288 | tf_op jit(solution)/shard_map/all_to_all | solution.py:171
  415.7 19.0 %all-to-all-start.6 = ((bf16[1,2,128,512]{3,1,0,2:T(2,128)(2,1)}), bf16[1,2,128,512]{3,1,0,2:T(2,128)(2,1)S(1)}, u32[]{:S(2)}, u32[]{:S(2)}) async-start(bf16[1,2,128,512]{3,1,0,2:T(2,128)(2,1)} %copy.99), calls=%async_computation.6 | async-start | bytes 524288 | tf_op jit(solution)/shard_map/all_to_all | solution.py:174
  434.6 18.8 %all-to-all-start.13 = ((bf16[1,2,128,1,512]{4,1,3,0,2:T(2,128)(2,1)}), bf16[1,2,128,1,512]{4,1,3,0,2:T(2,128)(2,1)S(1)}, u32[]{:S(2)}, u32[]{:S(2)}) async-start(bf16[1,2,128,1,512]{4,1,3,0,2:T(2,128)(2,1)} %copy.109), calls=%async_computation.13 | async-start | bytes 524288 | tf_op jit(solution)/shard_map/all_to_all | solution.py:191
  453.4 181.3 %all-to-all-start.7 = ((bf16[128,2,256]{2,1,0:T(2,128)(2,1)}), bf16[128,2,256]{2,1,0:T(2,128)(2,1)S(1)}, u32[]{:S(2)}, u32[]{:S(2)}) async-start(bf16[128,2,256]{2,1,0:T(2,128)(2,1)} %reshape.969), calls=%async_computation.7 | async-start | bytes 262144 | tf_op jit(solution)/shard_map/all_to_all | solution.py:191
  460.1 439.4 %all-reduce.2.cloned.1.call-start = ((), (), s32[]{:S(2)}) async-start(), calls=%async_computation.14 | async-start | bytes 1048576 | tf_op jit(solution)/shard_map/psum | solution.py:249
  634.7 0.9 copy-start.8
  634.7 1.0 copy-start.10
  634.7 1.0 copy-start.14
Sparse Core Ops, SparseCore 0:
  634.9 264.5 all-reduce.1
where the time goes:
time: 914 us; the launch traced here: 908 us
  other arithmetic  349 us (38%)
  waiting for transfers between devices  267 us (29%)
  starting transfers between devices  114 us (12%)
  blocking collectives  88.4 us (10%)
  local copies, waits for them, and re-layouts  41.6 us (5%)
  matrix products  31.4 us (3%)
  between operations  15.2 us (2%)
    psum x1, waiting for transfers between devices, on_device(): grad_coef, grad_skip = lax.psum((grad_local, skip_local), ('dp', 'seq'))  174 us
    reduce_sum x8, other arithmetic, coef_mode_step(): jnp.sum(weights[None] * wave_cos, axis=1)  163 us
    reduce_sum x8, other arithmetic, kernel_mode_step(): jnp.sum(coef_re[:, None, :] * wave_cos - coef_im[:, None, :] * wave_sin,...  158 us
    psum x1, blocking collectives, on_device(): grad_coef, grad_skip = lax.psum((grad_local, skip_local), ('dp', 'seq'))  88.4 us
    all_to_all x2, starting transfers between devices, signal_first(): lax.all_to_all(stacked[:, None], 'seq', split_axis=2, concat_axis=1, tile...  30 us
    all_to_all x3, starting transfers between devices, spectrum_turn(): lax.all_to_all(first_im.astype(jnp.bfloat16), 'seq', split_axis=1, concat...  26 us
    all_to_all x3, waiting for transfers between devices, spectrum_turn(): lax.all_to_all(first_im.astype(jnp.bfloat16), 'seq', split_axis=1, concat...  23.7 us
    all_to_all x2, waiting for transfers between devices, inverse_path(): lax.all_to_all(shortened(head_re), 'seq', split_axis=2, concat_axis=1, ti...  19.8 us
  transfers between devices with their start and end apart: 15, of which 12 were waited for; matrix products, arithmetic and copies ran while one was open for 44% of the time, Pallas kernels for 0%

commit v1 on v0

v1 whole, which is shorter than its diff:
```python
import math

import jax
import jax.numpy as jnp
import numpy as np
from jax import lax
from jax.sharding import PartitionSpec as P

highest = lax.Precision.HIGHEST
AXES = ("dp", "seq")


def tables(blocks, width):
    half = blocks
    period = 2 * blocks * width
    odd = 2 * np.arange(half) + 1
    angle = 2.0 * np.pi * (odd[:, None] * np.arange(2 * blocks)[None, :] % (4 * blocks)) / (4 * blocks)
    sign = np.where(np.arange(2 * blocks) < blocks, 1.0, -1.0)[None, :]
    outer = np.concatenate([np.cos(angle) * sign, -np.sin(angle) * sign], axis=0)
    angle = 2.0 * np.pi * (odd[:, None] * np.arange(width)[None, :]) / (2 * period)
    twist_cos, twist_sin = np.cos(angle), np.sin(angle)
    angle = 2.0 * np.pi * (np.arange(width)[:, None] * np.arange(width)[None, :] % width) / width
    cos, sin = np.cos(angle), np.sin(angle)
    inner = np.block([[cos, -sin], [sin, cos]])
    back = np.block([[cos, sin], [-sin, cos]])
    return [np.asarray(t, np.float32) for t in (outer, twist_cos, twist_sin, inner, back)]


def cos_turns(turns, length):
    quarter = length // 4
    v = (jnp.abs(turns - length // 2) - quarter).astype(jnp.float32) * (1.0 / quarter)
    w = v * v
    poly = 0.00015148419
    for c in (-0.00467376557, 0.07968967928, -0.64596371106, 1.57079631847):
        poly = poly * w + c
    return poly * v


def fade_table(rate, freq, lag, length, modes):
    lane = lax.broadcasted_iota(jnp.int32, (1, 2 * modes), 1)
    shift = jnp.where(lane < modes, 0, length - length // 4)
    turns = (freq * lag + shift) % length
    return jnp.exp(-rate * lag.astype(jnp.float32)) * cos_turns(turns, length)


def local_part(sig, cot, coef, rate, freq, skip, blocks, width):
    outer, twist_cos, twist_sin, inner, back = tables(blocks, width)
    channels, seqs = sig.shape[:2]
    length = blocks * width
    modes = rate.shape[1]
    scale = 2.0 * (modes * length) ** (-0.5)
    einsum = lambda *a: jnp.einsum(*a, precision=highest)

    def forward(x, table):
        a = einsum("ks,gsp->gkp", table, x)
        re, im = a[:, :blocks], a[:, blocks:]
        both = jnp.concatenate([re * twist_cos + im * twist_sin, im * twist_cos - re * twist_sin], axis=2)
        s = einsum("gkp,pq->gkq", both, inner)
        return s[:, :, :width], s[:, :, width:]

    def inverse(re, im, table):
        b = einsum("gkq,qp->gkp", jnp.concatenate([re, im], axis=2), back)
        re, im = b[:, :, :width], b[:, :, width:]
        both = jnp.concatenate([re * twist_cos - im * twist_sin, im * twist_cos + re * twist_sin], axis=1)
        return einsum("ks,gkp->gsp", table, both) * (1.0 / length)

    low = lax.broadcasted_iota(jnp.int32, (blocks, 1), 0)
    inn = lax.broadcasted_iota(jnp.int32, (width, 1), 0)
    lags = ((low * width, inn), ((blocks - 1 - low) * width, width - inn))
    live = jnp.where((low == 0) & (inn.T == 0), 0.0, 1.0)
    kern, fades = [], []
    for c in range(channels):
        halves = []
        for d in range(2):
            rate2 = jnp.tile(rate[d, :, c], 2)[None]
            freq2 = jnp.tile(freq[d, :, c], 2)[None]
            fa = fade_table(rate2, freq2, lags[d][0], length, modes)
            fb = fade_table(rate2, freq2, lags[d][1], length, modes)
            cre, cim = coef[d, 0, :, c], coef[d, 1, :, c]
            c1 = jnp.concatenate([cre, -cre])[None]
            c2 = jnp.concatenate([-cim, -cim])[None]
            mixed = c1 * fa + c2 * jnp.roll(fa, modes, axis=1)
            half = einsum("sn,pn->sp", mixed, fb) * scale
            halves.append(half if d == 0 else half * live)
            fades.append((fa, fb))
        kern.append(jnp.concatenate(halves, axis=0))
    kre, kim = forward(jnp.stack(kern), outer)
    flat = lambda t: t.reshape((channels * seqs, blocks, width)).astype(jnp.float32)
    sre, sim = forward(flat(sig), outer[:, :blocks])
    gre, gim = forward(flat(cot), outer[:, :blocks])
    kre, kim = (jnp.repeat(t, seqs, axis=0) for t in (kre, kim))
    out = inverse(gre * kre + gim * kim, gim * kre - gre * kim, outer[:, :blocks])
    corr = lambda t: t.reshape((channels, seqs, blocks, width)).sum(axis=1)
    wts = inverse(corr(gre * sre + gim * sim), corr(gim * sre - gre * sim), outer)
    out = out.reshape(cot.shape) + skip[:, None, None, None] * cot.astype(jnp.float32)
    rows = []
    for c in range(channels):
        for d in range(2):
            fa, fb = fades[c * 2 + d]
            w = wts[c, d * blocks:(d + 1) * blocks]
            if d:
                w = w * live
            t = einsum("sp,pn->sn", w, fb)
            p = jnp.sum(fa * t, axis=0)
            q = jnp.sum(fa * jnp.roll(t, modes, axis=1), axis=0)
            rows.append(jnp.concatenate([p[:modes] - p[modes:], -(q[:modes] + q[modes:])]) * scale)
    grads = jnp.stack(rows).reshape(channels, 2, 2, modes)
    skips = jnp.sum(flat(sig) * flat(cot), axis=(1, 2)).reshape(channels, seqs).sum(axis=1)
    return out.astype(jnp.bfloat16), grads, skips


def on_device(signal, grad_out, mode_coef, decay_param, freq_index, skip_gain):
    seq_count = lax.axis_size("seq")
    devices = lax.axis_size("dp") * seq_count
    width, channels = signal.shape[1:]
    each = channels // devices
    length = width * seq_count
    seqs = lax.axis_size("dp")
    mine = lax.axis_index(AXES) * each
    both = jnp.stack([signal[0], grad_out[0]]).transpose(2, 0, 1).reshape(devices, each, 2, width)
    got = lax.all_to_all(both, AXES, split_axis=0, concat_axis=0, tiled=True)
    got = got.reshape(seqs, seq_count, each, 2, width).transpose(3, 2, 0, 1, 4)
    take = lambda t: lax.dynamic_slice_in_dim(t, mine, each, t.ndim - 1)
    out, grads, skips = local_part(
        got[0], got[1], take(mode_coef), take(decay_param) / float(length), take(freq_index), take(skip_gain),
        seq_count, width)
    back = out.transpose(1, 2, 0, 3).reshape(devices, each, width)
    back = lax.all_to_all(back, AXES, split_axis=0, concat_axis=0, tiled=True)
    grad_signal = back.reshape(channels, width).T[None]
    flat = jnp.concatenate([grads.reshape(each, -1), skips[:, None]], axis=1)
    flat = lax.all_gather(flat, AXES, axis=0, tiled=True)
    grad_coef = flat[:, :-1].T.reshape(mode_coef.shape)
    return (grad_signal, grad_coef, flat[:, -1])


def solution(mesh):
    return jax.shard_map(
        on_device,
        mesh=mesh,
        in_specs=(P("dp", "seq", None), P("dp", "seq", None), P(), P(), P(), P()),
        out_specs=(P("dp", "seq", None), P(), P()),
        check_vma=False,
    )
```

time: 914 us -> 739 us (0.81)
  the two profiles are of different devices: /device:TPU:1 before, /device:TPU:128 now
where the time goes in v1:
time: 739 us; the launch traced here: 738 us
  blocking collectives  684 us (93%)
  starting transfers between devices  24.7 us (3%)
  local copies, waits for them, and re-layouts  11.6 us (2%)
  matrix products  9.9 us (1%)
    all_gather x1, blocking collectives, on_device(): flat = lax.all_gather(flat, AXES, axis=0, tiled=True)  684 us
  transfers between devices with their start and end apart: 2, of which 1 were waited for; matrix products, arithmetic and copies ran while one was open for 1% of the time, Pallas kernels for 0%

profile of v1, /device:TPU:128, one launch (start us, length us, event | category | flops | bytes accessed | tf_op | source)
XLA Modules:
  0.0 738.3 jit_solution(5669126125668385221)
XLA Ops:
  0.6 1.1 copy.76
  1.7 0.1 copy.75
  1.9 0.9 copy.77
  2.8 13.8 %all-to-all-start = ((bf16[256,2,2,128]{3,1,2,0:T(2,128)(2,1)}), bf16[256,2,2,128]{3,1,2,0:T(2,128)(2,1)S(1)}, u32[]{:S(2)}, u32[]{:S(2)}) async-start(bf16[256,2,2,128]{3,1,2,0:T(2,128)(2,1)} %copy.77), calls=%async_computation | async-start | bytes 524288 | tf_op jit(solution)/shard_map/all_to_all | solution.py:121
  16.7 0.2 dynamic-slice_reduce_fusion.6
  17.0 0.1 mul.779
  17.0 0.9 dynamic-slice_multiply_fusion
  18.0 0.2 fusion.137
  18.2 0.1 neg.119
  18.3 0.1 mul.844
  18.4 0.1 neg.131
  18.5 0.1 mul.873
  18.5 0.1 neg.137
  18.6 0.1 mul.812
  18.7 0.1 neg.125
  18.8 0.3 dynamic-slice_reduce_fusion.7
  19.2 0.4 multiply_multiply_fusion.21
  19.6 0.1 pad_maximum_fusion.8
  19.7 0.1 pad_maximum_fusion.6
  19.8 0.1 pad_maximum_fusion.4
  19.9 0.1 pad_maximum_fusion.2
  19.9 0.5 fusion.1
  20.4 0.5 fusion.2
  20.9 0.5 convolution_multiply_fusion.3
  21.4 0.5 convolution_multiply_fusion.5
  21.9 0.8 dynamic_slice.15
  22.7 0.9 copy-done.3
  23.6 0.6 convolution_bitcast_fusion.2
  24.2 2.8 all-to-all-done
  27.1 0.1 fusion.21
  27.2 0.8 copy-done.1
  28.0 0.4 convolution_bitcast_fusion
  28.4 0.4 convolution_bitcast_fusion.1
  28.9 0.4 copy-done.4
  29.3 0.1 multiply_add_fusion.1
  29.4 0.8 copy-done
  30.2 1.0 fusion.3
  31.2 1.0 fusion.14
  32.3 0.1 bitcast_reduce_fusion.1
  32.3 0.9 copy-done.2
  33.2 0.6 fusion.31
  33.9 0.6 fusion
  34.5 0.4 fusion.86
  34.9 0.4 fusion.87
  35.2 0.3 fusion.89
  35.6 0.3 fusion.88
  35.9 0.6 fusion.27
  36.6 0.7 fusion.7
  37.4 0.7 convolution_multiply_fusion.1
  38.1 0.1 fusion.20
  38.2 0.8 copy.87
  39.0 10.9 %all-to-all-start.1 = ((bf16[256,2,128]{2,1,0:T(2,128)(2,1)}), bf16[256,2,128]{2,1,0:T(2,128)(2,1)S(1)}, u32[]{:S(2)}, u32[]{:S(2)}) async-start(bf16[256,2,128]{2,1,0:T(2,128)(2,1)} %copy.87), calls=%async_computation.1 | async-start | bytes 262144 | tf_op jit(solution)/shard_map/all_to_all | solution.py:128
  49.9 0.1 copy.93
  50.0 0.3 multiply_reduce_fusion.2
  50.3 0.1 negate_bitcast_fusion
  50.5 0.3 multiply_reduce_fusion.3
  50.8 0.1 negate_bitcast_fusion.1
  51.3 0.1 maximum_multiply_fusion.11
  51.3 0.1 maximum_multiply_fusion.10
  51.6 683.6 %all-gather = f32[256,2,257]{2,1,0:T(2,128)S(1)} all-gather(f32[1,2,257]{2,1,0:T(2,128)S(1)} %maximum_bitcast_fusion.2), channel_id=1, replica_groups=mesh['dp'=2,'seq'=128] {'dp','seq'}, dimensions={0}, use_global_device_ids=true | all-gather | bytes 528392 | tf_op jit(solution)/shard_map/all_gather | solution.py:131
  735.2 0.5 reshape.280
  735.8 1.0 copy.94
  736.8 0.7 slice_reduce_fusion
  737.5 0.8 copy.95
  (61 shorter events, 1.2 us)
Async XLA Ops:
  0.6 1.1 copy-start.7
  1.9 14.8 %copy-start.8 = (s32[2,64,512]{2,1,0:T(8,128)S(1)}, s32[2,64,512]{2,1,0:T(8,128)}, u32[]{:S(2)}) copy-start(s32[2,64,512]{2,1,0:T(8,128)} %param.22) | copy-start | bytes 786436
  2.8 16.0 %copy-start.6 = (f32[2,2,64,512]{3,2,1,0:T(8,128)S(1)}, f32[2,2,64,512]{3,2,1,0:T(8,128)}, u32[]{:S(2)}) copy-start(f32[2,2,64,512]{3,2,1,0:T(8,128)} %param.20) | copy-start | bytes 1572868
  2.8 24.2 %all-to-all-start = ((bf16[256,2,2,128]{3,1,2,0:T(2,128)(2,1)}), bf16[256,2,2,128]{3,1,2,0:T(2,128)(2,1)S(1)}, u32[]{:S(2)}, u32[]{:S(2)}) async-start(bf16[256,2,2,128]{3,1,2,0:T(2,128)(2,1)} %copy.77), calls=%async_computation | async-start | bytes 524288 | tf_op jit(solution)/shard_map/all_to_all | solution.py:121
  22.6 0.9 copy-start.3
  27.1 0.9 copy-start.1
  28.4 0.8 copy-start.4
  28.4 0.9 copy-start.5
  29.3 0.9 copy-start
  32.3 1.0 copy-start.2
  39.0 698.6 %all-to-all-start.1 = ((bf16[256,2,128]{2,1,0:T(2,128)(2,1)}), bf16[256,2,128]{2,1,0:T(2,128)(2,1)S(1)}, u32[]{:S(2)}, u32[]{:S(2)}) async-start(bf16[256,2,128]{2,1,0:T(2,128)(2,1)} %copy.87), calls=%async_computation.1 | async-start | bytes 262144 | tf_op jit(solution)/shard_map/all_to_all | solution.py:128

commit v2 on v1

v2 whole, which is shorter than its diff:
```python
import functools
import math

import jax
import jax.numpy as jnp
import ml_dtypes
import numpy as np
from jax import lax
from jax.experimental import pallas as pl
from jax.experimental.pallas import tpu as pltpu
from jax.sharding import PartitionSpec as P

MESH = pl.DeviceIdType.MESH
F32, BF16 = jnp.float32, jnp.bfloat16


def tables(blocks, width):
    period = 2 * blocks * width
    odd = 2 * np.arange(blocks) + 1
    slot = np.arange(2 * blocks)
    angle = 2.0 * np.pi * (odd[:, None] * slot[None, :] % (4 * blocks)) / (4 * blocks)
    sign = np.where(slot < blocks, 1.0, -1.0)[None, :]
    outer = np.concatenate([np.cos(angle) * sign, -np.sin(angle) * sign], axis=0)
    angle = 2.0 * np.pi * (odd[:, None] * np.arange(width)[None, :]) / (2 * period)
    twist = np.stack([np.cos(angle), np.sin(angle)])
    spot = np.arange(width)
    angle = 2.0 * np.pi * (spot[:, None] * spot[None, :] % width) / width
    cos, sin = np.cos(angle), np.sin(angle)
    inner = np.block([[cos, -sin], [sin, cos]])
    back = np.block([[cos, sin], [-sin, cos]])
    mats = np.stack([outer, outer.T * (2.0 / period), inner, back])
    high = mats.astype(ml_dtypes.bfloat16)
    low = (mats - high.astype(np.float64)).astype(ml_dtypes.bfloat16)
    return np.stack([high, low], axis=1), twist.astype(np.float32)


def split(value):
    high = value.astype(BF16)
    return high, (value - high.astype(F32)).astype(BF16)


def dot(a, b):
    return jnp.dot(a, b, preferred_element_type=F32)


def dot3(a, b):
    return dot(a[0], b[0]) + dot(a[1], b[0]) + dot(a[0], b[1])


def fade_table(rate, freq, shift, lag, step, period):
    turns = freq * (lag * (1.0 / period)) + shift
    turns = turns - jnp.floor(turns)
    v = 4.0 * jnp.abs(turns - 0.5) - 1.0
    w = v * v
    poly = 0.00015148419 * w - 0.00467376557
    poly = poly * w + 0.07968967928
    poly = poly * w - 0.64596371106
    poly = poly * w + 1.57079631847
    return jnp.exp(-rate * (lag * step)) * (poly * v)


def kernel(n, modes, sig_ref, cot_ref, coef_ref, rate_ref, freq_ref, skip_ref, mat_ref, twist_ref,
           out_ref, gcoef_ref, gskip_ref,
           stage, send1, recv1, send2, recv2, kspec, through, corr_out, corr_own, corr_in, fades, direct,
           skip_mine, skip_mid, skip_all, skip_sum, skip_in, ssem, rsem):
    width = n
    core, me = lax.axis_index("dp"), lax.axis_index("seq")
    z, xy = lax.div(me, 16), lax.rem(me, 16)

    def remote(src, dst, k, seq=None):
        device = {"dp": 1 - core} if seq is None else {"seq": seq}
        return pltpu.make_async_remote_copy(
            src_ref=src, dst_ref=dst, send_sem=ssem.at[k], recv_sem=rsem.at[k], device_id=device,
            device_id_type=MESH)

    def finish(ref, k):
        pltpu.make_async_copy(ref, ref, ssem.at[k]).wait()
        pltpu.make_async_copy(ref, ref, rsem.at[k]).wait()

    barrier = pltpu.get_barrier_semaphore()

    def greet(i, c):
        pl.semaphore_signal(barrier, inc=1, device_id={"seq": lax.bitwise_xor(me, i)}, device_id_type=MESH)
        return c

    lax.fori_loop(1, n, greet, 0)
    pl.semaphore_signal(barrier, inc=1, device_id={"dp": 1 - core}, device_id_type=MESH)

    for k in range(8):
        src = (sig_ref, cot_ref)[k // 4]
        block = src[:, (k % 4) * width:(k % 4 + 1) * width].astype(F32)
        stage[pl.ds(k, n, stride=8), :] = block.T
    send1[...] = stage[...].reshape(n, 8, width).astype(BF16)

    pl.semaphore_wait(barrier, n)

    def post1(i, c):
        t = lax.bitwise_xor(me, i)
        remote(send1.at[t], recv1.at[me], 0, t).start()
        return c

    lax.fori_loop(1, n, post1, 0)
    recv1[me] = send1[me]

    lane = lax.broadcasted_iota(jnp.int32, (1, width), 1)
    wide = jnp.zeros((2 * modes, width), F32)
    slim = jnp.zeros((modes, width), F32)
    for j in range(4):
        for d in range(2):
            k = j * 2 + d
            cols = slice(j * width, (j + 1) * width)
            turn = lambda v, spot: pltpu.roll(v, lax.rem(spot + width - me, width), 1)
            wide = jnp.where(lane == k, turn(coef_ref[d, :, cols], k), wide)
            slim = jnp.where(lane == 8 + k, turn(rate_ref[d, :, cols], 8 + k), slim)
            slim = jnp.where(lane == 16 + k, turn(freq_ref[d, :, cols].astype(F32), 16 + k), slim)
    rows = jnp.where(lane < 8, wide, jnp.concatenate([slim, slim], axis=0)).T

    mat = lambda k: (mat_ref[k, 0], mat_ref[k, 1])
    outer, outer_t, inner, back = mat(0), mat(1), mat(2), mat(3)
    tcos, tsin = twist_ref[0], twist_ref[1]
    shift = jnp.where(lane < modes, 0.0, 0.75)
    spot = lax.broadcasted_iota(jnp.int32, (n, 1), 0).astype(F32)
    first = (lax.broadcasted_iota(jnp.int32, (n, width), 0) == 0) & (lax.broadcasted_iota(jnp.int32, (n, width), 1) == 0)
    scale = 2.0 * (modes * n * width) ** -0.5
    back_scale = scale

    def twisted(a):
        re, im = a[:n], a[n:]
        return jnp.concatenate([re * tcos + im * tsin, im * tcos - re * tsin], axis=1)

    for j in range(4):
        halves = []
        for d in range(2):
            k = j * 2 + d
            raw, rate, freq = rows[k:k + 1], rows[8 + k:9 + k] * (1.0 / (n * width)), rows[16 + k:17 + k]
            swap = jnp.concatenate([raw[:, modes:], raw[:, :modes]], axis=1)
            c1 = jnp.where(lane < modes, raw, -swap) * scale
            c2 = jnp.where(lane < modes, -swap, -raw) * scale
            fa = fade_table(rate, freq, shift, spot if d == 0 else (n - 1.0) - spot, float(width), float(n))
            fb = fade_table(rate, freq, shift, spot if d == 0 else width - spot, 1.0, float(n * width))
            fades[k, 0] = fa
            fades[k, 1] = fb
            mixed = c1 * fa + c2 * pltpu.roll(fa, modes, 1)
            a, b = split(mixed), split(fb)
            nt = lambda x, y: lax.dot_general(x, y, (((1,), (1,)), ((), ())), preferred_element_type=F32)
            half = nt(a[0], b[0]) + nt(a[1], b[0]) + nt(a[0], b[1])
            halves.append(half if d == 0 else jnp.where(first, 0.0, half))
        wave = jnp.concatenate(halves, axis=0)
        kspec[j] = dot3(split(twisted(dot3(outer, split(wave)))), inner)

    finish(recv1.at[pl.ds(0, n - 1)], 0)
    stage[...] = recv1[...].astype(F32).reshape(8 * n, width)
    outer_cat = jnp.concatenate([outer[0][:, :n], outer[1][:, :n]], axis=1)
    skip_row = jnp.zeros((1, width), F32)

    def channel(i, skip_row):
        j = lax.rem(2 * (1 - core) + i, 4)
        s = stage[pl.ds(j, n, stride=8), :]
        g = stage[pl.ds(j + 4, n, stride=8), :]
        total = jnp.sum(jnp.sum(s * g, axis=0, keepdims=True), axis=1, keepdims=True)
        skip_row = skip_row + jnp.where(lane == j, total, 0.0)
        x = jnp.concatenate([s, g], axis=1).astype(BF16)
        a = dot(outer_cat, jnp.concatenate([x, x], axis=0))
        both = jnp.concatenate([twisted(a[:, :width]), twisted(a[:, width:])], axis=0)
        spec = dot3(split(both), inner)
        sre, sim, gre, gim = spec[:n, :width], spec[:n, width:], spec[n:, :width], spec[n:, width:]
        kre, kim = kspec[j, :, :width], kspec[j, :, width:]
        through[j, :, :width] = gre * kre + gim * kim
        through[j, :, width:] = gim * kre - gre * kim
        corr_out[i, :, :width] = gre * sre + gim * sim
        corr_out[i, :, width:] = gim * sre - gre * sim
        gain = jnp.sum(jnp.where(lane == me, skip_ref[pl.ds(j, 1), :], 0.0), axis=1, keepdims=True)
        direct[j] = gain * g
        return skip_row

    skip_row = lax.fori_loop(0, 2, channel, skip_row)
    to_peer = remote(corr_out.at[pl.ds(0, 2)], corr_in, 1)
    to_peer.start()
    skip_row = lax.fori_loop(2, 4, channel, skip_row)

    skip_mine[...] = skip_row
    for i in range(1, 8):
        tz = lax.bitwise_xor(z, i)
        remote(skip_mine, skip_mid.at[z], 2, tz * 16 + xy).start()
    skip_mid[z] = skip_row

    def untwist(b):
        re, im = b[:, :width], b[:, width:]
        return jnp.concatenate([re * tcos - im * tsin, im * tcos + re * tsin], axis=0)

    b = dot3(split(through[...].reshape(4 * n, 2 * width)), back)
    cols = jnp.concatenate([untwist(b[j * n:(j + 1) * n]) for j in range(4)], axis=1)
    y = dot3((outer_t[0][:n], outer_t[1][:n]), split(cols))

    finish(skip_mid.at[pl.ds(0, 7)], 2)
    for i in range(1, 16):
        t = lax.bitwise_xor(xy, i)
        remote(skip_mid, skip_all.at[:, xy], 3, z * 16 + t).start()
    skip_all[:, xy] = skip_mid[...]

    to_peer.wait()
    corr = (corr_out[2:4] + corr_in[...]).reshape(2 * n, 2 * width)
    b = dot3(split(corr), back)
    cols = jnp.concatenate([untwist(b[:n]), untwist(b[n:])], axis=1)
    w = dot3(outer_t, split(cols))
    for jj in range(2):
        for d in range(2):
            k = (2 * core + jj) * 2 + d
            fa, fb = fades[k, 0], fades[k, 1]
            part = w[d * n:(d + 1) * n, jj * width:(jj + 1) * width]
            if d:
                part = jnp.where(first, 0.0, part)
            t = dot3(split(part), split(fb))
            p = jnp.sum(fa * t, axis=0, keepdims=True)
            q = jnp.sum(fa * pltpu.roll(t, modes, 1), axis=0, keepdims=True)
            p2 = jnp.concatenate([p[:, modes:], p[:, :modes]], axis=1)
            q2 = jnp.concatenate([q[:, modes:], q[:, :modes]], axis=1)
            row = jnp.where(lane < modes, p - p2, -(q + q2)) * back_scale
            stage[pl.ds(4 + jj * 2 + d, n, stride=8), :] = jnp.broadcast_to(row, (n, width))

    for j in range(4):
        stage[pl.ds(j, n, stride=8), :] = y[:, j * width:(j + 1) * width] + direct[j]
    send2[...] = stage[...].reshape(n, 8, width).astype(BF16)

    def post2(i, c):
        t = lax.bitwise_xor(me, i)
        remote(send2.at[t], recv2.at[me], 4, t).start()
        return c

    lax.fori_loop(1, n, post2, 0)
    recv2[me] = send2[me]

    finish(skip_all.at[:, pl.ds(0, 15)], 3)
    skip_sum[...] = skip_all[...].reshape(n, width).T[:8]
    skip_peer = remote(skip_sum, skip_in, 5)
    skip_peer.start()

    finish(recv2.at[pl.ds(0, n - 1)], 4)
    stage[...] = recv2[...].astype(F32).reshape(8 * n, width)
    for jj in range(2):
        for d in range(2):
            block = stage[pl.ds(4 + jj * 2 + d, n, stride=8), :].T
            gcoef_ref[d, :, pl.ds(pl.multiple_of((2 * core + jj) * width, width), width)] = block.astype(BF16)
    mine = gcoef_ref.at[:, :, pl.ds(pl.multiple_of(2 * core * width, 2 * width), 2 * width)]
    coef_peer = remote(mine, mine, 6)
    coef_peer.start()
    for j in range(4):
        out_ref[:, j * width:(j + 1) * width] = stage[pl.ds(j, n, stride=8), :].T.astype(BF16)
    skip_peer.wait()
    gskip_ref[...] = skip_sum[...] + skip_in[...]
    coef_peer.wait()


def on_device(signal, grad_out, mode_coef, decay_param, freq_index, skip_gain):
    n = lax.axis_size("seq")
    width, channels = signal.shape[1:]
    modes = decay_param.shape[1]
    mats, twist = tables(n, width)
    vmem = pl.BlockSpec(memory_space=pltpu.VMEM)
    out, gcoef, gskip = pl.pallas_call(
        functools.partial(kernel, n, modes),
        out_shape=(
            jax.ShapeDtypeStruct((width, channels), BF16),
            jax.ShapeDtypeStruct((2, 2 * modes, channels), BF16),
            jax.ShapeDtypeStruct((8, n), F32),
        ),
        in_specs=[vmem] * 8,
        out_specs=(vmem,) * 3,
        scratch_shapes=[
            pltpu.VMEM((8 * n, width), F32),
            pltpu.VMEM((n, 8, width), BF16),
            pltpu.VMEM((n, 8, width), BF16),
            pltpu.VMEM((n, 8, width), BF16),
            pltpu.VMEM((n, 8, width), BF16),
            pltpu.VMEM((4, n, 2 * width), F32),
            pltpu.VMEM((4, n, 2 * width), F32),
            pltpu.VMEM((4, n, 2 * width), F32),
            pltpu.VMEM((2, n, 2 * width), F32),
            pltpu.VMEM((2, n, 2 * width), F32),
            pltpu.VMEM((8, 2, n, 2 * modes), F32),
            pltpu.VMEM((4, n, width), F32),
            pltpu.VMEM((1, width), F32),
            pltpu.VMEM((8, 1, width), F32),
            pltpu.VMEM((8, 16, 1, width), F32),
            pltpu.VMEM((8, width), F32),
            pltpu.VMEM((8, width), F32),
            pltpu.SemaphoreType.DMA((8,)),
            pltpu.SemaphoreType.DMA((8,)),
        ],
        compiler_params=pltpu.CompilerParams(
            collective_id=0, has_side_effects=True, vmem_limit_bytes=40 * 1024 * 1024),
    )(signal[0], grad_out[0], mode_coef.reshape(2, 2 * modes, channels), decay_param, freq_index,
      skip_gain.reshape(channels // width, width), mats, twist)
    return (out[None], gcoef.astype(F32).reshape(mode_coef.shape), gskip[:channels // width].reshape(channels))


def solution(mesh):
    return jax.shard_map(
        on_device,
        mesh=mesh,
        in_specs=(P("dp", "seq", None), P("dp", "seq", None), P(), P(), P(), P()),
        out_specs=(P("dp", "seq", None), P(), P()),
        check_vma=False,
    )
```

time: 739 us -> 53.9 us (0.07)
  the two profiles are of different devices: /device:TPU:128 before, /device:TPU:1 now
where the time goes in v2:
time: 53.9 us; the launch traced here: 53.6 us
  Pallas kernels  43.3 us (80%)
  local copies, waits for them, and re-layouts  8.79 us (16%)
  other arithmetic  0.85 us (2%)
  between operations  0.66 us (1%)
    pallas_call x1, Pallas kernels, on_device(): pl.pallas_call(functools.partial(kernel, n, modes), out_shape=(jax.ShapeD...  43.3 us
    unnamed x17, local copies, waits for them, and re-layouts  8.2 us

profile of v2, /device:TPU:1, one launch (start us, length us, event | category | flops | bytes accessed | tf_op | source)
XLA Modules:
  0.0 53.6 jit_solution(14928987799110347475)
XLA Ops:
  0.6 0.0 copy-start.7
  0.6 0.7 %copy-done.7 = f32[512]{0:T(512)S(1)} copy-done((f32[512]{0:T(512)S(1)}, f32[512]{0:T(512)}, u32[]{:S(2)}) %copy-start.7) | copy-done | bytes 2072
  1.3 0.0 copy-start
  1.3 1.2 %copy-done = bf16[4,2,256,256]{3,2,1,0:T(8,128)(2,1)S(1)} copy-done((bf16[4,2,256,256]{3,2,1,0:T(8,128)(2,1)S(1)}, bf16[4,2,256,256]{3,2,1,0:T(8,128)(2,1)}, u32[]{:S(2)}) %copy-start) | copy-done | bytes 1048600
  2.5 0.0 copy-start.1
  2.5 1.0 %copy-done.1 = f32[2,2,64,512]{3,2,1,0:T(8,128)S(1)} copy-done((f32[2,2,64,512]{3,2,1,0:T(8,128)S(1)}, f32[2,2,64,512]{3,2,1,0:T(8,128)}, u32[]{:S(2)}) %copy-start.1) | copy-done | bytes 524312
  3.6 0.0 copy-start.2
  3.6 0.9 %copy-done.2 = f32[2,64,512]{2,1,0:T(8,128)S(1)} copy-done((f32[2,64,512]{2,1,0:T(8,128)S(1)}, f32[2,64,512]{2,1,0:T(8,128)}, u32[]{:S(2)}) %copy-start.2) | copy-done | bytes 262168
  4.5 0.0 copy-start.3
  4.5 0.9 %copy-done.3 = s32[2,64,512]{2,1,0:T(8,128)S(1)} copy-done((s32[2,64,512]{2,1,0:T(8,128)S(1)}, s32[2,64,512]{2,1,0:T(8,128)}, u32[]{:S(2)}) %copy-start.3) | copy-done | bytes 262168
  5.5 0.0 copy-start.4
  5.5 0.9 %copy-done.4 = bf16[1,128,512]{2,1,0:T(8,128)(2,1)S(1)} copy-done((bf16[1,128,512]{2,1,0:T(8,128)(2,1)S(1)}, bf16[1,128,512]{2,1,0:T(8,128)(2,1)}, u32[]{:S(2)}) %copy-start.4) | copy-done | bytes 131096
  6.4 0.0 copy-start.5
  6.4 0.9 %copy-done.5 = bf16[1,128,512]{2,1,0:T(8,128)(2,1)S(1)} copy-done((bf16[1,128,512]{2,1,0:T(8,128)(2,1)S(1)}, bf16[1,128,512]{2,1,0:T(8,128)(2,1)}, u32[]{:S(2)}) %copy-start.5) | copy-done | bytes 131096
  7.3 0.0 copy-start.6
  7.3 0.9 %copy-done.6 = f32[2,128,128]{2,1,0:T(8,128)S(1)} copy-done((f32[2,128,128]{2,1,0:T(8,128)S(1)}, f32[2,128,128]{2,1,0:T(8,128)}, u32[]{:S(2)}) %copy-start.6) | copy-done | bytes 131096
  8.2 43.3 %shard_map.103 = (bf16[128,512]{1,0:T(8,128)(2,1)S(1)}, bf16[2,128,512]{2,1,0:T(8,128)(2,1)S(1)}, f32[8,128]{1,0:T(8,128)S(1)}) custom-call(bf16[128,512]{1,0:T(8,128)(2,1)S(1)} %bitcast.11, bf16[128,512]{1,0:T(8,128)(2,1)S(1)} %bitcast.12, f32[2,128,512]{2,1,0:T(8,128)S(1)} %bitcast.9, f32[2,64,512]{2,1,0:T(8,128)S(1)} %copy-done.2, ...), custom_call_target="tpu_custom_call" | custom-call | tf_op jit(solution)/shard_map/pallas_call | solution.py:260
  51.5 0.6 %slice_bitcast_fusion = f32[512]{0:T(512)} fusion(f32[8,128]{1,0:T(8,128)S(1)} %get-tuple-element.8), kind=kLoop, calls=%fused_computation | loop fusion | bytes 4096 | tf_op jit(solution)/shard_map/reshape | solution.py:294
  52.1 0.9 %convert.1 = f32[2,2,64,512]{3,2,1,0:T(8,128)} convert(bf16[2,2,64,512]{3,2,1,0:T(8,128)(2,1)S(1)} %bitcast.10) | non-fusion elementwise | flops 131072 | bytes 786432 | tf_op jit(solution)/shard_map/reshape | solution.py:294
  52.9 0.7 %copy.12 = bf16[1,128,512]{2,1,0:T(8,128)(2,1)} copy(bf16[1,128,512]{2,1,0:T(8,128)(2,1)S(1)} %bitcast.13) | data formatting | bytes 262144
Async XLA Ops:
  0.6 0.7 %copy-start.7 = (f32[512]{0:T(512)S(1)}, f32[512]{0:T(512)}, u32[]{:S(2)}) copy-start(f32[512]{0:T(512)} %param.13) | copy-start | bytes 6148
  1.3 1.2 %copy-start = (bf16[4,2,256,256]{3,2,1,0:T(8,128)(2,1)S(1)}, bf16[4,2,256,256]{3,2,1,0:T(8,128)(2,1)}, u32[]{:S(2)}) copy-start(bf16[4,2,256,256]{3,2,1,0:T(8,128)(2,1)} %constant.4.clone.mat_ref) | copy-start | bytes 3145732
  2.5 1.0 %copy-start.1 = (f32[2,2,64,512]{3,2,1,0:T(8,128)S(1)}, f32[2,2,64,512]{3,2,1,0:T(8,128)}, u32[]{:S(2)}) copy-start(f32[2,2,64,512]{3,2,1,0:T(8,128)} %param.10) | copy-start | bytes 1572868
  3.6 0.9 %copy-start.2 = (f32[2,64,512]{2,1,0:T(8,128)S(1)}, f32[2,64,512]{2,1,0:T(8,128)}, u32[]{:S(2)}) copy-start(f32[2,64,512]{2,1,0:T(8,128)} %rate_ref.1) | copy-start | bytes 786436
  4.5 0.9 %copy-start.3 = (s32[2,64,512]{2,1,0:T(8,128)S(1)}, s32[2,64,512]{2,1,0:T(8,128)}, u32[]{:S(2)}) copy-start(s32[2,64,512]{2,1,0:T(8,128)} %freq_ref.1) | copy-start | bytes 786436
  5.5 0.9 %copy-start.4 = (bf16[1,128,512]{2,1,0:T(8,128)(2,1)S(1)}, bf16[1,128,512]{2,1,0:T(8,128)(2,1)}, u32[]{:S(2)}) copy-start(bf16[1,128,512]{2,1,0:T(8,128)(2,1)} %param.8) | copy-start | bytes 393220
  6.4 0.9 %copy-start.5 = (bf16[1,128,512]{2,1,0:T(8,128)(2,1)S(1)}, bf16[1,128,512]{2,1,0:T(8,128)(2,1)}, u32[]{:S(2)}) copy-start(bf16[1,128,512]{2,1,0:T(8,128)(2,1)} %param.9) | copy-start | bytes 393220
  7.3 0.9 %copy-start.6 = (f32[2,128,128]{2,1,0:T(8,128)S(1)}, f32[2,128,128]{2,1,0:T(8,128)}, u32[]{:S(2)}) copy-start(f32[2,128,128]{2,1,0:T(8,128)} %constant.5.clone.twist_ref) | copy-start | bytes 393220

commit v3 on v2

--- a/solution.py
+++ b/solution.py
@@ -1,5 +1,4 @@
 import functools
-import math
 
 import jax
 import jax.numpy as jnp
@@ -12,6 +11,8 @@
 
 MESH = pl.DeviceIdType.MESH
 F32, BF16 = jnp.float32, jnp.bfloat16
+ROOM = 62 * 1024 * 1024
+UNROLL = 8
 
 
 def tables(blocks, width):
@@ -59,13 +60,21 @@
     return jnp.exp(-rate * (lag * step)) * (poly * v)
 
 
-def kernel(n, modes, sig_ref, cot_ref, coef_ref, rate_ref, freq_ref, skip_ref, mat_ref, twist_ref,
+def kernel(n, modes, sig_in, cot_in, coef_in, rate_in, freq_in, gain_in, mat_in, twist_in,
            out_ref, gcoef_ref, gskip_ref,
-           stage, send1, recv1, send2, recv2, kspec, through, corr_out, corr_own, corr_in, fades, direct,
-           skip_mine, skip_mid, skip_all, skip_sum, skip_in, ssem, rsem):
+           sig_ref, cot_ref, coef_ref, rate_ref, freq_ref, gain_ref, mat_ref, twist_ref, lsem,
+           stage, stage2, send1, recv1, send2, recv2, kspec, through, corr_out, corr_in, fades, direct,
+           gmid, gall, skip_sum, skip_in, ssem, rsem):
     width = n
     core, me = lax.axis_index("dp"), lax.axis_index("seq")
     z, xy = lax.div(me, 16), lax.rem(me, 16)
+
+    loads = [
+        pltpu.make_async_copy(src, dst, lsem.at[k]) for k, (src, dst) in enumerate((
+            (sig_in, sig_ref), (cot_in, cot_ref), (coef_in, coef_ref), (rate_in, rate_ref), (freq_in, freq_ref),
+            (gain_in, gain_ref), (mat_in, mat_ref), (twist_in, twist_ref)))]
+    for load in loads:
+        load.start()
 
     def remote(src, dst, k, seq=None):
         device = {"dp": 1 - core} if seq is None else {"seq": seq}
@@ -83,9 +92,11 @@
         pl.semaphore_signal(barrier, inc=1, device_id={"seq": lax.bitwise_xor(me, i)}, device_id_type=MESH)
         return c
 
-    lax.fori_loop(1, n, greet, 0)
+    lax.fori_loop(1, n, greet, 0, unroll=UNROLL)
     pl.semaphore_signal(barrier, inc=1, device_id={"dp": 1 - core}, device_id_type=MESH)
 
+    loads[0].wait()
+    loads[1].wait()
     for k in range(8):
         src = (sig_ref, cot_ref)[k // 4]
         block = src[:, (k % 4) * width:(k % 4 + 1) * width].astype(F32)
@@ -99,9 +110,11 @@
         remote(send1.at[t], recv1.at[me], 0, t).start()
         return c
 
-    lax.fori_loop(1, n, post1, 0)
+    lax.fori_loop(1, n, post1, 0, unroll=UNROLL)
     recv1[me] = send1[me]
 
+    for load in loads[2:]:
+        load.wait()
     lane = lax.broadcasted_iota(jnp.int32, (1, width), 1)
     wide = jnp.zeros((2 * modes, width), F32)
     slim = jnp.zeros((modes, width), F32)
@@ -120,13 +133,17 @@
     tcos, tsin = twist_ref[0], twist_ref[1]
     shift = jnp.where(lane < modes, 0.0, 0.75)
     spot = lax.broadcasted_iota(jnp.int32, (n, 1), 0).astype(F32)
-    first = (lax.broadcasted_iota(jnp.int32, (n, width), 0) == 0) & (lax.broadcasted_iota(jnp.int32, (n, width), 1) == 0)
+    first = (lax.broadcasted_iota(jnp.int32, (n, width), 0) == 0) & (
+        lax.broadcasted_iota(jnp.int32, (n, width), 1) == 0)
     scale = 2.0 * (modes * n * width) ** -0.5
-    back_scale = scale
 
     def twisted(a):
         re, im = a[:n], a[n:]
         return jnp.concatenate([re * tcos + im * tsin, im * tcos - re * tsin], axis=1)
+
+    def untwist(b):
+        re, im = b[:, :width], b[:, width:]
+        return jnp.concatenate([re * tcos - im * tsin, im * tcos + re * tsin], axis=0)
 
     for j in range(4):
         halves = []
@@ -151,7 +168,6 @@
     finish(recv1.at[pl.ds(0, n - 1)], 0)
     stage[...] = recv1[...].astype(F32).reshape(8 * n, width)
     outer_cat = jnp.concatenate([outer[0][:, :n], outer[1][:, :n]], axis=1)
-    skip_row = jnp.zeros((1, width), F32)
 
     def channel(i, skip_row):
         j = lax.rem(2 * (1 - core) + i, 4)
@@ -169,40 +185,30 @@
         through[j, :, width:] = gim * kre - gre * kim
         corr_out[i, :, :width] = gre * sre + gim * sim
         corr_out[i, :, width:] = gim * sre - gre * sim
-        gain = jnp.sum(jnp.where(lane == me, skip_ref[pl.ds(j, 1), :], 0.0), axis=1, keepdims=True)
+        gain = jnp.sum(jnp.where(lane == me, gain_ref[pl.ds(j, 1), :], 0.0), axis=1, keepdims=True)
         direct[j] = gain * g
         return skip_row
 
-    skip_row = lax.fori_loop(0, 2, channel, skip_row)
+    skip_row = jnp.zeros((1, width), F32)
+    for i in range(2):
+        skip_row = channel(i, skip_row)
     to_peer = remote(corr_out.at[pl.ds(0, 2)], corr_in, 1)
     to_peer.start()
-    skip_row = lax.fori_loop(2, 4, channel, skip_row)
-
-    skip_mine[...] = skip_row
-    for i in range(1, 8):
-        tz = lax.bitwise_xor(z, i)
-        remote(skip_mine, skip_mid.at[z], 2, tz * 16 + xy).start()
-    skip_mid[z] = skip_row
-
-    def untwist(b):
-        re, im = b[:, :width], b[:, width:]
-        return jnp.concatenate([re * tcos - im * tsin, im * tcos + re * tsin], axis=0)
+    for i in range(2, 4):
+        skip_row = channel(i, skip_row)
 
     b = dot3(split(through[...].reshape(4 * n, 2 * width)), back)
     cols = jnp.concatenate([untwist(b[j * n:(j + 1) * n]) for j in range(4)], axis=1)
     y = dot3((outer_t[0][:n], outer_t[1][:n]), split(cols))
-
-    finish(skip_mid.at[pl.ds(0, 7)], 2)
-    for i in range(1, 16):
-        t = lax.bitwise_xor(xy, i)
-        remote(skip_mid, skip_all.at[:, xy], 3, z * 16 + t).start()
-    skip_all[:, xy] = skip_mid[...]
+    for j in range(4):
+        send2[:, j, :] = (y[:, j * width:(j + 1) * width] + direct[j]).astype(BF16)
 
     to_peer.wait()
     corr = (corr_out[2:4] + corr_in[...]).reshape(2 * n, 2 * width)
     b = dot3(split(corr), back)
     cols = jnp.concatenate([untwist(b[:n]), untwist(b[n:])], axis=1)
     w = dot3(outer_t, split(cols))
+    grads = []
     for jj in range(2):
         for d in range(2):
             k = (2 * core + jj) * 2 + d
@@ -215,40 +221,52 @@
             q = jnp.sum(fa * pltpu.roll(t, modes, 1), axis=0, keepdims=True)
             p2 = jnp.concatenate([p[:, modes:], p[:, :modes]], axis=1)
             q2 = jnp.concatenate([q[:, modes:], q[:, :modes]], axis=1)
-            row = jnp.where(lane < modes, p - p2, -(q + q2)) * back_scale
-            stage[pl.ds(4 + jj * 2 + d, n, stride=8), :] = jnp.broadcast_to(row, (n, width))
-
-    for j in range(4):
-        stage[pl.ds(j, n, stride=8), :] = y[:, j * width:(j + 1) * width] + direct[j]
-    send2[...] = stage[...].reshape(n, 8, width).astype(BF16)
+            grads.append(jnp.where(lane < modes, p - p2, -(q + q2)) * scale)
+    skip_high = skip_row.astype(BF16).astype(F32)
+    blank = jnp.zeros((2, width), F32)
+    gmid[z] = jnp.concatenate(grads + [skip_high, skip_row - skip_high, blank], axis=0).astype(BF16)
+
+    for i in range(1, 8):
+        remote(gmid.at[z], gmid.at[z], 2, lax.bitwise_xor(z, i) * 16 + xy).start()
 
     def post2(i, c):
         t = lax.bitwise_xor(me, i)
         remote(send2.at[t], recv2.at[me], 4, t).start()
         return c
 
-    lax.fori_loop(1, n, post2, 0)
+    lax.fori_loop(64, n, post2, 0, unroll=UNROLL)
+    finish(gmid.at[pl.ds(0, 7)], 2)
+    for i in range(1, 16):
+        remote(gmid, gall.at[:, xy], 3, z * 16 + lax.bitwise_xor(xy, i)).start()
+    lax.fori_loop(1, 64, post2, 0, unroll=UNROLL)
     recv2[me] = send2[me]
-
-    finish(skip_all.at[:, pl.ds(0, 15)], 3)
-    skip_sum[...] = skip_all[...].reshape(n, width).T[:8]
+    gall[:, xy] = gmid[...]
+
+    finish(gall.at[:, pl.ds(0, 15)], 3)
+    stage2[...] = gall[...].astype(F32).reshape(8 * n, width)
+    skip_sum[...] = (stage2[pl.ds(4, n, stride=8), :] + stage2[pl.ds(5, n, stride=8), :]).T[:4]
+    for jj in range(2):
+        for d in range(2):
+            block = stage2[pl.ds(jj * 2 + d, n, stride=8), :].T
+            gcoef_ref[d, :, pl.ds(pl.multiple_of((2 * core + jj) * width, width), width)] = block.astype(BF16)
     skip_peer = remote(skip_sum, skip_in, 5)
     skip_peer.start()
-
-    finish(recv2.at[pl.ds(0, n - 1)], 4)
-    stage[...] = recv2[...].astype(F32).reshape(8 * n, width)
-    for jj in range(2):
-        for d in range(2):
-            block = stage[pl.ds(4 + jj * 2 + d, n, stride=8), :].T
-            gcoef_ref[d, :, pl.ds(pl.multiple_of((2 * core + jj) * width, width), width)] = block.astype(BF16)
     mine = gcoef_ref.at[:, :, pl.ds(pl.multiple_of(2 * core * width, 2 * width), 2 * width)]
     coef_peer = remote(mine, mine, 6)
     coef_peer.start()
+
+    finish(recv2.at[pl.ds(0, n - 1)], 4)
     for j in range(4):
-        out_ref[:, j * width:(j + 1) * width] = stage[pl.ds(j, n, stride=8), :].T.astype(BF16)
+        out_ref[:, j * width:(j + 1) * width] = recv2[:, j, :].astype(F32).T.astype(BF16)
     skip_peer.wait()
     gskip_ref[...] = skip_sum[...] + skip_in[...]
     coef_peer.wait()
+
+
+def finals(out_in, gcoef_in, gskip_in, out_ref, gcoef_ref, gskip_ref):
+    out_ref[...] = out_in[...]
+    gcoef_ref[...] = gcoef_in[...].astype(F32)
+    gskip_ref[...] = gskip_in[...]
 
 
 def on_device(signal, grad_out, mode_coef, decay_param, freq_index, skip_gain):
@@ -257,41 +275,49 @@
     modes = decay_param.shape[1]
     mats, twist = tables(n, width)
     vmem = pl.BlockSpec(memory_space=pltpu.VMEM)
-    out, gcoef, gskip = pl.pallas_call(
+    operands = (signal[0], grad_out[0], mode_coef.reshape(2, 2 * modes, channels), decay_param, freq_index,
+                skip_gain.reshape(channels // width, width), mats, twist)
+    out = pl.pallas_call(
         functools.partial(kernel, n, modes),
         out_shape=(
             jax.ShapeDtypeStruct((width, channels), BF16),
             jax.ShapeDtypeStruct((2, 2 * modes, channels), BF16),
-            jax.ShapeDtypeStruct((8, n), F32),
+            jax.ShapeDtypeStruct((channels // width, n), F32),
         ),
-        in_specs=[vmem] * 8,
+        in_specs=[pl.BlockSpec(memory_space=pl.ANY)] * 8,
         out_specs=(vmem,) * 3,
-        scratch_shapes=[
+        scratch_shapes=[pltpu.VMEM(t.shape, t.dtype) for t in operands] + [
+            pltpu.SemaphoreType.DMA((8,)),
+            pltpu.VMEM((8 * n, width), F32),
             pltpu.VMEM((8 * n, width), F32),
             pltpu.VMEM((n, 8, width), BF16),
             pltpu.VMEM((n, 8, width), BF16),
-            pltpu.VMEM((n, 8, width), BF16),
-            pltpu.VMEM((n, 8, width), BF16),
+            pltpu.VMEM((n, 4, width), BF16),
+            pltpu.VMEM((n, 4, width), BF16),
             pltpu.VMEM((4, n, 2 * width), F32),
             pltpu.VMEM((4, n, 2 * width), F32),
             pltpu.VMEM((4, n, 2 * width), F32),
             pltpu.VMEM((2, n, 2 * width), F32),
-            pltpu.VMEM((2, n, 2 * width), F32),
             pltpu.VMEM((8, 2, n, 2 * modes), F32),
             pltpu.VMEM((4, n, width), F32),
-            pltpu.VMEM((1, width), F32),
-            pltpu.VMEM((8, 1, width), F32),
-            pltpu.VMEM((8, 16, 1, width), F32),
-            pltpu.VMEM((8, width), F32),
-            pltpu.VMEM((8, width), F32),
+            pltpu.VMEM((8, 8, width), BF16),
+            pltpu.VMEM((8, 16, 8, width), BF16),
+            pltpu.VMEM((4, width), F32),
+            pltpu.VMEM((4, width), F32),
             pltpu.SemaphoreType.DMA((8,)),
             pltpu.SemaphoreType.DMA((8,)),
         ],
         compiler_params=pltpu.CompilerParams(
-            collective_id=0, has_side_effects=True, vmem_limit_bytes=40 * 1024 * 1024),
-    )(signal[0], grad_out[0], mode_coef.reshape(2, 2 * modes, channels), decay_param, freq_index,
-      skip_gain.reshape(channels // width, width), mats, twist)
-    return (out[None], gcoef.astype(F32).reshape(mode_coef.shape), gskip[:channels // width].reshape(channels))
+            collective_id=0, has_side_effects=True, vmem_limit_bytes=ROOM),
+    )(*operands)
+    out = pl.pallas_call(
+        finals,
+        out_shape=tuple(jax.ShapeDtypeStruct(t.shape, d) for t, d in zip(out, (BF16, F32, F32))),
+        in_specs=[vmem] * 3,
+        out_specs=(vmem,) * 3,
+        compiler_params=pltpu.CompilerParams(vmem_limit_bytes=ROOM),
+    )(*out)
+    return (out[0][None], out[1].reshape(mode_coef.shape), out[2].reshape(channels))
 
 
 def solution(mesh):

time: 53.9 us -> 45.1 us (0.84)
  local copies, waits for them, and re-layouts: 8.79 us -> 0 us
  Pallas kernels: 43.3 us -> 44.4 us
  other arithmetic: 0.85 us -> 0 us
    unnamed x17 -> x0, local copies, waits for them, and re-layouts: 8.2 us -> none
    pallas_call x0 -> x1, Pallas kernels: none -> 1.87 us  [on_device(): pl.pallas_call(finals, out_shape=tuple((jax.ShapeDtypeStruct(t.shape, d)...]
    reshape x1 -> x0, other arithmetic: 0.85 us -> none  [on_device(): gcoef.astype(F32).reshape(mode_coef.shape)]
    pallas_call x1, Pallas kernels: 43.3 us -> 42.5 us  [on_device(): pl.pallas_call(functools.partial(kernel, n, modes), out_shape=(jax.ShapeD...]
    reshape x1 -> x0, local copies, waits for them, and re-layouts: 0.58 us -> none  [on_device(): gskip[:channels // width].reshape(channels)]
where the time goes in v3:
time: 45.1 us; the launch traced here: 45 us
  Pallas kernels  44.4 us (98%)
  between operations  0.64 us (1%)
    pallas_call x1, Pallas kernels, on_device(): pl.pallas_call(functools.partial(kernel, n, modes), out_shape=(jax.ShapeD...  42.5 us
    pallas_call x1, Pallas kernels, on_device(): pl.pallas_call(finals, out_shape=tuple((jax.ShapeDtypeStruct(t.shape, d)...  1.87 us

profile of v3, /device:TPU:1, one launch (start us, length us, event | category | flops | bytes accessed | tf_op | source)
XLA Modules:
  0.0 45.0 jit_solution(11663942710047856010)
XLA Ops:
  0.6 42.5 %shard_map.103 = (bf16[128,512]{1,0:T(8,128)(2,1)}, bf16[2,128,512]{2,1,0:T(8,128)(2,1)}, f32[4,128]{1,0:T(4,128)}) custom-call(bf16[128,512]{1,0:T(8,128)(2,1)} %bitcast.8, bf16[128,512]{1,0:T(8,128)(2,1)} %bitcast.9, f32[2,128,512]{2,1,0:T(8,128)} %bitcast.7, f32[2,64,512]{2,1,0:T(8,128)} %rate_in.1, s32[2,64,512]{2,1,0:T(8,128)} %freq_in.1, ...), custom_call_target="tpu_custom_call" | custom-call | tf_op jit(solution)/shard_map/pallas_call | solution.py:280
  43.2 1.9 %shard_map.104 = (bf16[128,512]{1,0:T(8,128)(2,1)}, f32[2,128,512]{2,1,0:T(8,128)}, f32[4,128]{1,0:T(4,128)}) custom-call(bf16[128,512]{1,0:T(8,128)(2,1)} %get-tuple-element.9.out_in, bf16[2,128,512]{2,1,0:T(8,128)(2,1)} %get-tuple-element.10.gcoef_in, f32[4,128]{1,0:T(4,128)} %get-tuple-element.11.gskip_in), custom_call_target="tpu_custom_call" | custom-call | tf_op jit(solution)/shard_map/pallas_call | solution.py:313

commit v4 on v3

--- a/solution.py
+++ b/solution.py
@@ -13,6 +13,7 @@
 F32, BF16 = jnp.float32, jnp.bfloat16
 ROOM = 62 * 1024 * 1024
 UNROLL = 8
+FAR_FIRST = (4, 5, 3, 7, 2, 6, 1, 0)
 
 
 def tables(blocks, width):
@@ -64,7 +65,7 @@
            out_ref, gcoef_ref, gskip_ref,
            sig_ref, cot_ref, coef_ref, rate_ref, freq_ref, gain_ref, mat_ref, twist_ref, lsem,
            stage, stage2, send1, recv1, send2, recv2, kspec, through, corr_out, corr_in, fades, direct,
-           gmid, gall, skip_sum, skip_in, ssem, rsem):
+           gmid, gsend, gall, ssem, rsem):
     width = n
     core, me = lax.axis_index("dp"), lax.axis_index("seq")
     z, xy = lax.div(me, 16), lax.rem(me, 16)
@@ -76,8 +77,10 @@
     for load in loads:
         load.start()
 
-    def remote(src, dst, k, seq=None):
-        device = {"dp": 1 - core} if seq is None else {"seq": seq}
+    def remote(src, dst, k, seq=None, other=False):
+        device = {} if seq is None else {"seq": seq}
+        if other:
+            device["dp"] = 1 - core
         return pltpu.make_async_remote_copy(
             src_ref=src, dst_ref=dst, send_sem=ssem.at[k], recv_sem=rsem.at[k], device_id=device,
             device_id_type=MESH)
@@ -93,7 +96,9 @@
         return c
 
     lax.fori_loop(1, n, greet, 0, unroll=UNROLL)
-    pl.semaphore_signal(barrier, inc=1, device_id={"dp": 1 - core}, device_id_type=MESH)
+    for i in range(8):
+        pl.semaphore_signal(
+            barrier, inc=1, device_id={"dp": 1 - core, "seq": lax.bitwise_xor(z, i) * 16 + xy}, device_id_type=MESH)
 
     loads[0].wait()
     loads[1].wait()
@@ -103,14 +108,15 @@
         stage[pl.ds(k, n, stride=8), :] = block.T
     send1[...] = stage[...].reshape(n, 8, width).astype(BF16)
 
-    pl.semaphore_wait(barrier, n)
+    pl.semaphore_wait(barrier, n + 7)
 
     def post1(i, c):
         t = lax.bitwise_xor(me, i)
         remote(send1.at[t], recv1.at[me], 0, t).start()
         return c
 
-    lax.fori_loop(1, n, post1, 0, unroll=UNROLL)
+    for q in FAR_FIRST:
+        lax.fori_loop(max(16 * q, 1), 16 * q + 16, post1, 0, unroll=UNROLL)
     recv1[me] = send1[me]
 
     for load in loads[2:]:
@@ -192,16 +198,10 @@
     skip_row = jnp.zeros((1, width), F32)
     for i in range(2):
         skip_row = channel(i, skip_row)
-    to_peer = remote(corr_out.at[pl.ds(0, 2)], corr_in, 1)
+    to_peer = remote(corr_out.at[pl.ds(0, 2)], corr_in, 1, None, True)
     to_peer.start()
     for i in range(2, 4):
         skip_row = channel(i, skip_row)
-
-    b = dot3(split(through[...].reshape(4 * n, 2 * width)), back)
-    cols = jnp.concatenate([untwist(b[j * n:(j + 1) * n]) for j in range(4)], axis=1)
-    y = dot3((outer_t[0][:n], outer_t[1][:n]), split(cols))
-    for j in range(4):
-        send2[:, j, :] = (y[:, j * width:(j + 1) * width] + direct[j]).astype(BF16)
 
     to_peer.wait()
     corr = (corr_out[2:4] + corr_in[...]).reshape(2 * n, 2 * width)
@@ -224,43 +224,59 @@
             grads.append(jnp.where(lane < modes, p - p2, -(q + q2)) * scale)
     skip_high = skip_row.astype(BF16).astype(F32)
     blank = jnp.zeros((2, width), F32)
-    gmid[z] = jnp.concatenate(grads + [skip_high, skip_row - skip_high, blank], axis=0).astype(BF16)
+    slot = core * 8 + z
+    gmid[slot] = jnp.concatenate(grads + [skip_high, skip_row - skip_high, blank], axis=0).astype(BF16)
 
     for i in range(1, 8):
-        remote(gmid.at[z], gmid.at[z], 2, lax.bitwise_xor(z, i) * 16 + xy).start()
+        for other in (False, True):
+            remote(gmid.at[slot], gmid.at[slot], 2, lax.bitwise_xor(z, i) * 16 + xy, other).start()
+    remote(gmid.at[slot], gmid.at[slot], 2, None, True).start()
+    b = dot3(split(through[...].reshape(4 * n, 2 * width)), back)
+    cols = jnp.concatenate([untwist(b[j * n:(j + 1) * n]) for j in range(4)], axis=1)
+    y = dot3((outer_t[0][:n], outer_t[1][:n]), split(cols))
+    for j in range(4):
+        stage2[pl.ds(j, n, stride=4), :] = y[:, j * width:(j + 1) * width] + direct[j]
+    send2[...] = stage2[:4 * n].reshape(n, 4, width).astype(BF16)
 
     def post2(i, c):
         t = lax.bitwise_xor(me, i)
         remote(send2.at[t], recv2.at[me], 4, t).start()
         return c
 
-    lax.fori_loop(64, n, post2, 0, unroll=UNROLL)
-    finish(gmid.at[pl.ds(0, 7)], 2)
+    for q in FAR_FIRST[:8]:
+        lax.fori_loop(max(16 * q, 1), 16 * q + 16, post2, 0, unroll=UNROLL)
+    finish(gmid.at[pl.ds(0, 15)], 2)
+    seen = gmid[...].astype(F32)
+    gsend[pl.ds(0, 16)] = seen[:, :4].astype(BF16)
+    skips = jnp.zeros((2, width), F32)
+    for q in range(8):
+        part = seen[q, 4:5] + seen[q, 5:6] + (seen[8 + q, 4:5] + seen[8 + q, 5:6])
+        part = pltpu.roll(part, 4 * q, 1) if q else part
+        high = part.astype(BF16).astype(F32)
+        skips = skips + jnp.concatenate([high, part - high], axis=0)
+    gsend[16] = jnp.concatenate([skips, blank], axis=0).astype(BF16)
     for i in range(1, 16):
-        remote(gmid, gall.at[:, xy], 3, z * 16 + lax.bitwise_xor(xy, i)).start()
-    lax.fori_loop(1, 64, post2, 0, unroll=UNROLL)
+        remote(gsend, gall.at[xy], 3, z * 16 + lax.bitwise_xor(xy, i)).start()
+    for q in FAR_FIRST[8:]:
+        lax.fori_loop(max(16 * q, 1), 16 * q + 16, post2, 0, unroll=UNROLL)
     recv2[me] = send2[me]
-    gall[:, xy] = gmid[...]
-
-    finish(gall.at[:, pl.ds(0, 15)], 3)
-    stage2[...] = gall[...].astype(F32).reshape(8 * n, width)
-    skip_sum[...] = (stage2[pl.ds(4, n, stride=8), :] + stage2[pl.ds(5, n, stride=8), :]).T[:4]
-    for jj in range(2):
-        for d in range(2):
-            block = stage2[pl.ds(jj * 2 + d, n, stride=8), :].T
-            gcoef_ref[d, :, pl.ds(pl.multiple_of((2 * core + jj) * width, width), width)] = block.astype(BF16)
-    skip_peer = remote(skip_sum, skip_in, 5)
-    skip_peer.start()
-    mine = gcoef_ref.at[:, :, pl.ds(pl.multiple_of(2 * core * width, 2 * width), 2 * width)]
-    coef_peer = remote(mine, mine, 6)
-    coef_peer.start()
-
+    gall[xy] = gsend[...]
+
+    finish(gall.at[pl.ds(0, 15)], 3)
+    stage2[...] = gall[...].astype(F32).reshape(17 * 64, width)
+    skips = (stage2[pl.ds(64, 16, stride=68), :] + stage2[pl.ds(65, 16, stride=68), :]).T
+    gskip_ref[...] = jnp.concatenate([skips[4 * q:4 * q + 4] for q in range(8)], axis=1)
+    for c in range(2):
+        for jj in range(2):
+            for d in range(2):
+                block = jnp.concatenate([
+                    stage2[pl.ds((8 * c + q) * 4 + jj * 2 + d, 16, stride=68), :] for q in range(8)], axis=0).T
+                cols = slice((2 * c + jj) * width, (2 * c + jj + 1) * width)
+                gcoef_ref[d, :, cols] = block.astype(BF16)
     finish(recv2.at[pl.ds(0, n - 1)], 4)
+    stage[:4 * n] = recv2[...].astype(F32).reshape(4 * n, width)
     for j in range(4):
-        out_ref[:, j * width:(j + 1) * width] = recv2[:, j, :].astype(F32).T.astype(BF16)
-    skip_peer.wait()
-    gskip_ref[...] = skip_sum[...] + skip_in[...]
-    coef_peer.wait()
+        out_ref[:, j * width:(j + 1) * width] = stage[pl.ds(j, n, stride=4), :].T.astype(BF16)
 
 
 def finals(out_in, gcoef_in, gskip_in, out_ref, gcoef_ref, gskip_ref):
@@ -289,7 +305,7 @@
         scratch_shapes=[pltpu.VMEM(t.shape, t.dtype) for t in operands] + [
             pltpu.SemaphoreType.DMA((8,)),
             pltpu.VMEM((8 * n, width), F32),
-            pltpu.VMEM((8 * n, width), F32),
+            pltpu.VMEM((17 * 64, width), F32),
             pltpu.VMEM((n, 8, width), BF16),
             pltpu.VMEM((n, 8, width), BF16),
             pltpu.VMEM((n, 4, width), BF16),
@@ -300,10 +316,9 @@
             pltpu.VMEM((2, n, 2 * width), F32),
             pltpu.VMEM((8, 2, n, 2 * modes), F32),
             pltpu.VMEM((4, n, width), F32),
-            pltpu.VMEM((8, 8, width), BF16),
-            pltpu.VMEM((8, 16, 8, width), BF16),
-            pltpu.VMEM((4, width), F32),
-            pltpu.VMEM((4, width), F32),
+            pltpu.VMEM((16, 8, width), BF16),
+            pltpu.VMEM((17, 4, width), BF16),
+            pltpu.VMEM((16, 17, 4, width), BF16),
             pltpu.SemaphoreType.DMA((8,)),
             pltpu.SemaphoreType.DMA((8,)),
         ],

time: 45.1 us -> 42.4 us (0.940)
  Pallas kernels: 44.4 us -> 41.6 us
    pallas_call x1, Pallas kernels: 42.5 us -> 39.8 us  [on_device(): pl.pallas_call(functools.partial(kernel, n, modes), out_shape=(jax.ShapeD...]
where the time goes in v4:
time: 42.4 us; the launch traced here: 42.3 us
  Pallas kernels  41.6 us (98%)
  between operations  0.64 us (2%)
    pallas_call x1, Pallas kernels, on_device(): pl.pallas_call(functools.partial(kernel, n, modes), out_shape=(jax.ShapeD...  39.8 us
    pallas_call x1, Pallas kernels, on_device(): pl.pallas_call(finals, out_shape=tuple((jax.ShapeDtypeStruct(t.shape, d)...  1.87 us

profile of v4, /device:TPU:1, one launch (start us, length us, event | category | flops | bytes accessed | tf_op | source)
XLA Modules:
  0.0 42.3 jit_solution(12409192530923789036)
XLA Ops:
  0.6 39.8 %shard_map.103 = (bf16[128,512]{1,0:T(8,128)(2,1)}, bf16[2,128,512]{2,1,0:T(8,128)(2,1)}, f32[4,128]{1,0:T(4,128)}) custom-call(bf16[128,512]{1,0:T(8,128)(2,1)} %bitcast.8, bf16[128,512]{1,0:T(8,128)(2,1)} %bitcast.9, f32[2,128,512]{2,1,0:T(8,128)} %bitcast.7, f32[2,64,512]{2,1,0:T(8,128)} %rate_in.1, s32[2,64,512]{2,1,0:T(8,128)} %freq_in.1, ...), custom_call_target="tpu_custom_call" | custom-call | tf_op jit(solution)/shard_map/pallas_call | solution.py:296
  40.4 1.9 %shard_map.104 = (bf16[128,512]{1,0:T(8,128)(2,1)}, f32[2,128,512]{2,1,0:T(8,128)}, f32[4,128]{1,0:T(4,128)}) custom-call(bf16[128,512]{1,0:T(8,128)(2,1)} %get-tuple-element.9.out_in, bf16[2,128,512]{2,1,0:T(8,128)(2,1)} %get-tuple-element.10.gcoef_in, f32[4,128]{1,0:T(4,128)} %get-tuple-element.11.gskip_in), custom_call_target="tpu_custom_call" | custom-call | tf_op jit(solution)/shard_map/pallas_call | solution.py:328

commit v5 on v4

--- a/solution.py
+++ b/solution.py
@@ -262,6 +262,10 @@
     recv2[me] = send2[me]
     gall[xy] = gsend[...]
 
+    finish(recv2.at[pl.ds(0, n - 1)], 4)
+    stage[:4 * n] = recv2[...].astype(F32).reshape(4 * n, width)
+    for j in range(4):
+        out_ref[:, j * width:(j + 1) * width] = stage[pl.ds(j, n, stride=4), :].T.astype(BF16)
     finish(gall.at[pl.ds(0, 15)], 3)
     stage2[...] = gall[...].astype(F32).reshape(17 * 64, width)
     skips = (stage2[pl.ds(64, 16, stride=68), :] + stage2[pl.ds(65, 16, stride=68), :]).T
@@ -273,16 +277,27 @@
                     stage2[pl.ds((8 * c + q) * 4 + jj * 2 + d, 16, stride=68), :] for q in range(8)], axis=0).T
                 cols = slice((2 * c + jj) * width, (2 * c + jj + 1) * width)
                 gcoef_ref[d, :, cols] = block.astype(BF16)
-    finish(recv2.at[pl.ds(0, n - 1)], 4)
-    stage[:4 * n] = recv2[...].astype(F32).reshape(4 * n, width)
-    for j in range(4):
-        out_ref[:, j * width:(j + 1) * width] = stage[pl.ds(j, n, stride=4), :].T.astype(BF16)
-
-
-def finals(out_in, gcoef_in, gskip_in, out_ref, gcoef_ref, gskip_ref):
-    out_ref[...] = out_in[...]
-    gcoef_ref[...] = gcoef_in[...].astype(F32)
-    gskip_ref[...] = gskip_in[...]
+
+
+def finals(out_in, gcoef_in, gskip_in, out, gcoef, gskip, low, wide, y, sem):
+    copy = lambda src, dst, k: pltpu.make_async_copy(src, dst, sem.at[k])
+    rows = low.shape[1] // 2
+    parts = [(d, pl.ds(h * rows, rows)) for d in range(2) for h in range(2)]
+    loads = [copy(gcoef_in.at[p], low.at[p], k) for k, p in enumerate(parts)]
+    moves = [copy(gskip_in, gskip, 9)]
+    load_y = copy(out_in, y, 8)
+    for move in [load_y] + loads + moves:
+        move.start()
+    load_y.wait()
+    moves.append(copy(y, out, 10))
+    moves[-1].start()
+    for k, p in enumerate(parts):
+        loads[k].wait()
+        wide[p] = low[p].astype(F32)
+        moves.append(copy(wide.at[p], gcoef.at[p], 4 + k))
+        moves[-1].start()
+    for move in moves:
+        move.wait()
 
 
 def on_device(signal, grad_out, mode_coef, decay_param, freq_index, skip_gain):
@@ -325,11 +340,18 @@
         compiler_params=pltpu.CompilerParams(
             collective_id=0, has_side_effects=True, vmem_limit_bytes=ROOM),
     )(*operands)
+    hbm = pl.BlockSpec(memory_space=pl.ANY)
     out = pl.pallas_call(
         finals,
         out_shape=tuple(jax.ShapeDtypeStruct(t.shape, d) for t, d in zip(out, (BF16, F32, F32))),
-        in_specs=[vmem] * 3,
-        out_specs=(vmem,) * 3,
+        in_specs=[hbm] * 3,
+        out_specs=(hbm,) * 3,
+        scratch_shapes=[
+            pltpu.VMEM(out[1].shape, BF16),
+            pltpu.VMEM(out[1].shape, F32),
+            pltpu.VMEM(out[0].shape, BF16),
+            pltpu.SemaphoreType.DMA((11,)),
+        ],
         compiler_params=pltpu.CompilerParams(vmem_limit_bytes=ROOM),
     )(*out)
     return (out[0][None], out[1].reshape(mode_coef.shape), out[2].reshape(channels))

time: 42.4 us -> 42.3 us (level)
  no operation moved by 1% of the time
where the time goes in v5:
time: 42.3 us; the launch traced here: 42.1 us
  Pallas kernels  41.5 us (98%)
  between operations  0.64 us (2%)
    pallas_call x1, Pallas kernels, on_device(): pl.pallas_call(functools.partial(kernel, n, modes), out_shape=(jax.ShapeD...  39.7 us
    pallas_call x1, Pallas kernels, on_device(): pl.pallas_call(finals, out_shape=tuple((jax.ShapeDtypeStruct(t.shape, d)...  1.83 us

profile of v5, /device:TPU:1, one launch (start us, length us, event | category | flops | bytes accessed | tf_op | source)
XLA Modules:
  0.0 42.1 jit_solution(14671849009711296460)
XLA Ops:
  0.6 39.7 %shard_map.103 = (bf16[128,512]{1,0:T(8,128)(2,1)}, bf16[2,128,512]{2,1,0:T(8,128)(2,1)}, f32[4,128]{1,0:T(4,128)}) custom-call(bf16[128,512]{1,0:T(8,128)(2,1)} %bitcast.8, bf16[128,512]{1,0:T(8,128)(2,1)} %bitcast.9, f32[2,128,512]{2,1,0:T(8,128)} %bitcast.7, f32[2,64,512]{2,1,0:T(8,128)} %rate_in.1, s32[2,64,512]{2,1,0:T(8,128)} %freq_in.1, ...), custom_call_target="tpu_custom_call" | custom-call | tf_op jit(solution)/shard_map/pallas_call | solution.py:311
  40.3 1.8 %shard_map.104 = (bf16[128,512]{1,0:T(8,128)(2,1)}, f32[2,128,512]{2,1,0:T(8,128)}, f32[4,128]{1,0:T(4,128)}) custom-call(bf16[128,512]{1,0:T(8,128)(2,1)} %get-tuple-element.9.out_in, bf16[2,128,512]{2,1,0:T(8,128)(2,1)} %get-tuple-element.10.gcoef_in, f32[4,128]{1,0:T(4,128)} %get-tuple-element.11.gskip_in), custom_call_target="tpu_custom_call" | custom-call | tf_op jit(solution)/shard_map/pallas_call | solution.py:344
